TPU v7x, 256 devices: a whole 4x4x8 slice. The times are simulated.
256 devices in a mesh: row: 8 (over y_hi, x), col: 32 (over z, y_lo, core).
Axes of the slice: x: 4, y: 4 (y_hi: 2, y_lo: 2; y = y_hi * 2 + y_lo), z: 8, core: 2. Of those that a mesh axis runs over, the one named last changes fastest.
Arguments:
- pair_field: float32 [512, 512, 128], P('row', 'col'), may hold values from -6 to 6
- token_mask: int32 [512], replicated, may hold values 0 or 1
- norm_in_gain: float32 [2, 128], replicated, may hold values from 0.1 to 1.9
- norm_in_shift: float32 [2, 128], replicated, may hold values from -3 to 3
- proj_in: bfloat16 [2, 128, 256], replicated, may hold values from -0.5 to 0.5
- gate_in: bfloat16 [2, 128, 256], replicated, may hold values from -0.5 to 0.5
- norm_out_gain: float32 [2, 128], replicated, may hold values from 0.1 to 1.9
- norm_out_shift: float32 [2, 128], replicated, may hold values from -3 to 3
- gate_out: bfloat16 [2, 128, 128], replicated, may hold values from -0.5 to 0.5
- proj_out: bfloat16 [2, 128, 128], replicated, may hold values from -0.5 to 0.5
Outputs:
- updated: float32 [512, 512, 128], P('row', 'col')
All inputs are finite; a program needn't handle non-finite values.
Results may differ from a plain program's by a relative error of at most 0.007.
Values may be sent and summed in bfloat16 or wider, within the bound.
No kernel may reach another device: no remote copies, remote signals or barrier semaphores. Data moves between devices by JAX's collectives and lax.ppermute only.
A program may use at most 128 MiB of HBM per device.

v0:
```python
import functools

import jax
import jax.numpy as jnp
import numpy as np
from jax import lax
from jax.experimental import pallas as pl
from jax.experimental.pallas import tpu as pltpu
from jax.sharding import Mesh
from jax.sharding import PartitionSpec as P

EPSILON = 1e-05
ROWS, LANES, HALF = 8, 128, 64
BF, F32 = jnp.bfloat16, jnp.float32
VMEM_LIMIT = 40 * 1024 * 1024
ORDER = ("z", "y", "h", "x")
LISTS = {"z": (6, 2, 7, 3, 0, 4, 1, 5), "y": (0, 1), "h": (1, 0), "x": (2, 3, 0, 1)}


def sigmoid(x):
    return 0.5 * jnp.tanh(0.5 * x) + 0.5


def layer_norm(values, gain, shift, axis):
    average = jnp.mean(values, axis=axis, keepdims=True)
    centred = values - average
    spread = jnp.mean(centred * centred, axis=axis, keepdims=True)
    return centred * lax.rsqrt(spread + EPSILON) * gain + shift


def low_lanes(shape):
    return lax.broadcasted_iota(jnp.int32, shape, len(shape) - 1) < HALF


def swap_halves(first, second):
    low, axis = low_lanes(first.shape), first.ndim - 1
    return (
        jnp.where(low, first, pltpu.roll(second, HALF, axis)),
        jnp.where(low, pltpu.roll(first, HALF, axis), second),
    )


def project(chunk, s, weight, gain, shift, weights, staged, normed_ref):
    normed = layer_norm(chunk, gain, shift, -1).astype(BF)
    normed_ref[s : s + 2] = normed.reshape(2, LANES, LANES)
    both = lax.dot_general(weights, normed, (((1,), (1,)), ((), ())), preferred_element_type=F32)
    halves = sigmoid(both[2 * LANES :]) * both[: 2 * LANES] * weight
    for n in range(2):
        part = halves[:, n * LANES : (n + 1) * LANES]
        staged[pl.ds(s + n, LANES, stride=2 * ROWS), :] = part[:LANES]
        staged[pl.ds(ROWS + s + n, LANES, stride=2 * ROWS), :] = part[LANES:]


def joined_weights(proj_in, gate_in):
    return jnp.concatenate([proj_in.T, gate_in.T], axis=0)


def pair_of(ref, s):
    return ref[s : s + 2].reshape(2 * LANES, LANES)


def residual(prior_ref, gates_ref, proj_out, wide, columns_ref, layer, s):
    parts = [wide[pl.ds(s + n, LANES, stride=ROWS), :] for n in range(2)]
    gain, shift = (jnp.concatenate([columns_ref[layer, n]] * 2, axis=1) for n in range(2))
    mixed = layer_norm(jnp.concatenate(parts, axis=1), gain, shift, 0).astype(BF)
    update = lax.dot_general(mixed, proj_out, (((0,), (0,)), ((), ())), preferred_element_type=F32)
    return pair_of(prior_ref, s) + pair_of(gates_ref, s) * update


def tokens_of(pair_ref, s):
    return jnp.concatenate(
        [pair_ref[pl.ds(b * ROWS + s, HALF, stride=2 * ROWS), :] for b in range(2)], axis=0
    )


def first_kernel(
    pair_hbm, mask_hbm, lanes_hbm, gain_hbm, shift_hbm, out_gain_hbm, out_shift_hbm, proj_hbm, gate_hbm,
    send_ref, normed_ref, weight_ref, vectors_ref,
    pair_ref, mask_vec, mask_smem, gain, shift, out_gain, out_shift, proj_in, gate_in, staged, arrived,
):
    moves = [
        (proj_hbm.at[0], proj_in),
        (gate_hbm.at[0], gate_in),
        (pair_hbm, pair_ref),
        (mask_hbm, mask_smem),
        (lanes_hbm, mask_vec),
        (gain_hbm, gain),
        (shift_hbm, shift),
        (out_gain_hbm, out_gain),
        (out_shift_hbm, out_shift),
    ]
    copies = [
        pltpu.make_async_copy(src, dst, arrived.at[n]) for n, (src, dst) in enumerate(moves)
    ]
    for copy in copies:
        copy.start()
    for copy in copies[:2]:
        copy.wait()
    weights = joined_weights(proj_in[...], gate_in[...])
    for copy in copies[2:]:
        copy.wait()
    row, core = lax.axis_index(("h", "x")), lax.axis_index("core")
    chip = lax.axis_index("z") * 2 + lax.axis_index("y")
    low = low_lanes((1, LANES))
    tokens = mask_vec[pl.ds(row // 2, 1), :].astype(F32)
    own = jnp.where(low == (row % 2 == 0), tokens, pltpu.roll(tokens, HALF, 1))
    begin = (chip * 2 + core) * (2 * ROWS)
    for s in range(0, ROWS, 2):
        both = []
        for n in range(2):
            first = mask_smem[begin + s + n].astype(F32)
            second = mask_smem[begin + ROWS + s + n].astype(F32)
            weight = own * jnp.where(low, first, second)
            weight_ref[pl.ds(s + n, 1), :] = weight
            both.append(weight)
        chunk = jnp.concatenate([tokens_of(pair_ref, s), tokens_of(pair_ref, s + 1)], axis=0)
        weight = jnp.concatenate(both, axis=1)
        project(chunk, s, weight, gain[0:1], shift[0:1], weights, staged, normed_ref)
    send_ref[...] = staged[...].astype(BF).reshape(send_ref.shape)
    for n, ref in enumerate((gain, shift, out_gain, out_shift)):
        vectors_ref[pl.ds(2 * n, 2), :] = ref[...]


def gates_of(normed_ref, gate_out, gates_ref):
    for s in range(0, ROWS, 2):
        gating = jnp.dot(pair_of(normed_ref, s), gate_out[0], preferred_element_type=F32)
        gates_ref[s : s + 2] = sigmoid(gating).reshape(2, LANES, LANES)


def second_kernel(
    back_ref, prior_ref, gates_ref, weights_ref, columns_ref, weight_ref, vectors_ref, proj_out,
    send_ref, normed_ref, pass_ref, staged, wide,
):
    wide[...] = back_ref[...].astype(F32).reshape(wide.shape)
    gain, shift = vectors_ref[pl.ds(1, 1), :], vectors_ref[pl.ds(3, 1), :]
    for s in range(0, ROWS, 2):
        first_pass = residual(prior_ref, gates_ref, proj_out[0], wide, columns_ref, 0, s)
        pass_ref[s : s + 2] = first_pass.reshape(2, LANES, LANES)
        weight = jnp.concatenate([weight_ref[pl.ds(s + n, 1), :] for n in range(2)], axis=1)
        project(first_pass, s, weight, gain, shift, weights_ref[...], staged, normed_ref)
    send_ref[...] = staged[...].astype(BF).reshape(send_ref.shape)


def third_kernel(back_ref, pass_ref, gates_ref, columns_ref, proj_out, out_ref, wide):
    wide[...] = back_ref[...].astype(F32).reshape(wide.shape)
    for s in range(0, ROWS, 2):
        updated = residual(pass_ref, gates_ref, proj_out[0], wide, columns_ref, 1, s)
        for n in range(4):
            place = n % 2 * ROWS + s + n // 2
            out_ref[pl.ds(place, HALF, stride=2 * ROWS), :] = updated[n * HALF : (n + 1) * HALF]


def of_row(row, wide_x):
    at = {"h": LISTS["h"].index(row // wide_x), "x": LISTS["x"].index(row % wide_x)}
    return tuple(at.get(axis, slice(None)) for axis in ORDER)


def columns_first(block):
    if ORDER.index("z") > ORDER.index("y"):
        block = jnp.swapaxes(block, 0, 1)
    zs, ys = ([LISTS[axis].index(n) for n in range(len(LISTS[axis]))] for axis in "zy")
    return jnp.stack([jnp.stack([block[z, y] for y in ys]) for z in zs])


def as_listed(block):
    block = jnp.stack([jnp.stack([block[z, y] for y in LISTS["y"]]) for z in LISTS["z"]])
    return jnp.swapaxes(block, 0, 1) if ORDER.index("z") > ORDER.index("y") else block


def gather_rows(ref, half, store):
    wide_x = ref.shape[ORDER.index("x")]
    rows = slice(half * ROWS, (half + 1) * ROWS)
    for m in range(ROWS // 2):
        first = columns_first(ref[of_row(2 * m, wide_x)].astype(F32))
        second = columns_first(ref[of_row(2 * m + 1, wide_x)].astype(F32))
        low, high = swap_halves(first[:, :, rows], second[:, :, rows])
        store(pl.ds(m * LANES, LANES), jnp.concatenate([low, high], axis=2).astype(BF))


def scatter_rows(product, out_ref):
    wide_x = out_ref.shape[ORDER.index("x")]
    for m in range(ROWS // 2):
        part = product[..., m * LANES : (m + 1) * LANES]
        even, odd = swap_halves(part[:, :, :ROWS], part[:, :, ROWS:])
        out_ref[of_row(2 * m, wide_x)] = as_listed(even.astype(BF))
        out_ref[of_row(2 * m + 1, wide_x)] = as_listed(odd.astype(BF))


def keep_in(ref):
    def store(lanes, tile):
        ref[:, :, :, lanes] = tile

    return store


def outgoing_product(ref, left, right, total):
    gather_rows(ref, 0, keep_in(left))
    gather_rows(ref, 1, keep_in(right))
    tokens = left.shape[-1]
    lefts, rights = left[...].reshape(-1, tokens), right[...].reshape(-1, tokens)
    total[...] = lax.dot_general(
        rights, lefts, (((0,), (0,)), ((), ())), preferred_element_type=F32
    ).reshape(total.shape)
    return total[:, :, lax.axis_index("core")]


def outgoing_own_kernel(
    own_ref, pair_ref, normed_ref, gate_out, proj_in, gate_in, vectors_ref,
    partial_ref, prior_ref, gates_ref, weights_ref, columns_ref, left, right, total,
):
    partial_ref[...] = outgoing_product(own_ref, left, right, total)
    gates_of(normed_ref, gate_out, gates_ref)
    for s in range(ROWS):
        prior_ref[s] = tokens_of(pair_ref, s)
    weights_ref[...] = joined_weights(proj_in[0], gate_in[0])
    for layer in range(2):
        for n in range(2):
            row_vec = vectors_ref[pl.ds(4 + 2 * n + layer, 1), :]
            columns_ref[layer, n] = jnp.broadcast_to(row_vec, (LANES, LANES)).T


def outgoing_kernel(other_ref, partial_ref, out_ref, left, right, total):
    scatter_rows(partial_ref[...] + outgoing_product(other_ref, left, right, total), out_ref)


def incoming_own_kernel(own_ref, normed_ref, gate_out, left_ref, right_ref, gates_ref):
    gather_rows(own_ref, 0, keep_in(left_ref))
    gather_rows(own_ref, 1, keep_in(right_ref))
    gates_of(normed_ref, gate_out, gates_ref)


def incoming_kernel(other_ref, left_ref, right_ref, out_ref, left):
    core = lax.axis_index("core")
    left[:, :, core] = left_ref[...]

    def store(lanes, tile):
        left[:, :, 1 - core, :, lanes] = tile

    gather_rows(other_ref, 0, store)
    tokens = left.shape[-1]
    lefts, rights = left[...].reshape(-1, tokens), right_ref[...].reshape(-1, tokens)
    product = lax.dot_general(rights, lefts, (((1,), (1,)), ((), ())), preferred_element_type=F32)
    scatter_rows(product.reshape(right_ref.shape), out_ref)


def whole(shape):
    return pl.BlockSpec(shape, lambda i: (0,) * len(shape))


def layer_of(array, layer):
    return pl.BlockSpec((1, *array.shape[1:]), lambda i: (layer, 0, 0))


HBM = pl.BlockSpec(memory_space=pltpu.HBM)


def call(body, in_specs, out_shapes, scratch, name, flops=None):
    cost = None
    if flops is not None:
        cost = pl.CostEstimate(flops=flops, bytes_accessed=4 * 2**20, transcendentals=2**17)
    return pl.pallas_call(
        body,
        grid=(1,),
        in_specs=in_specs,
        out_specs=[whole(o.shape) for o in out_shapes],
        out_shape=out_shapes,
        scratch_shapes=scratch,
        compiler_params=pltpu.CompilerParams(vmem_limit_bytes=VMEM_LIMIT),
        cost_estimate=cost,
        name=name,
    )


def on_device(chips, pair_field, token_mask, gain, shift, proj_in, gate_in, out_gain, out_shift, gate_out, proj_out):
    tokens = pair_field.shape[0] * pair_field.shape[1]
    channels = pair_field.shape[2]
    pairs = pair_field.reshape(tokens, channels)
    mask_vec = token_mask.reshape(-1, LANES)
    axes = ("h", "x", "z", "y", "core")
    sizes = {axis: lax.axis_size(axis) for axis in axes}
    by_chip = tuple(sizes[axis] for axis in ORDER)
    places = np.arange(2 * chips).reshape([sizes[axis] for axis in axes])
    places = places[np.ix_(*(LISTS.get(axis, range(2)) for axis in axes))]
    places = places.transpose([axes.index(axis) for axis in (*ORDER, "core")])
    groups = places.reshape(chips, 2).T.tolist()
    n = token_mask.shape[0]
    own_columns = (sizes["z"], 2, 2 * ROWS, n)
    all_columns = (sizes["z"], 2, 2, 2 * ROWS, n)

    shape = jax.ShapeDtypeStruct
    send = shape((chips, 2 * ROWS, LANES), BF)
    sent_by_chip = shape(by_chip + send.shape[1:], BF)
    back = shape((chips, ROWS, LANES), BF)
    back_by_chip = shape(by_chip + back.shape[1:], BF)
    kept = shape((ROWS, LANES, channels), BF)
    kept_wide = shape(kept.shape, F32)
    joined = shape((4 * channels, channels), BF)
    columns = shape((2, 2, channels, LANES), F32)
    rows = shape((ROWS, LANES), F32)
    staged = pltpu.VMEM((channels * 2 * ROWS, LANES), F32)
    wide = pltpu.VMEM((channels * ROWS, LANES), F32)
    own_half = pltpu.VMEM(own_columns, BF)
    total = pltpu.VMEM(all_columns, F32)
    flops = 2 * tokens * channels * channels

    def exchange(x):
        return lax.all_to_all(x, axes, 0, 0, axis_index_groups=groups, tiled=True)

    def triangle(sent, own_call, own_operands, other_call):
        mine = exchange(sent)
        mine, *own_operands = lax.optimization_barrier([mine, *own_operands])
        other = lax.ppermute(mine, "core", [(0, 1), (1, 0)])
        made = own_call(mine.reshape(sent_by_chip.shape), *own_operands)
        other, made = lax.optimization_barrier((other, made))
        result, aside = other_call(other.reshape(sent_by_chip.shape), made)
        return exchange(result.reshape(back.shape)), aside

    sent, normed, weights, vectors = call(
        first_kernel,
        [HBM] * 9,
        [send, kept, rows, rows],
        [
            pltpu.VMEM(pairs.shape, F32),
            pltpu.VMEM(mask_vec.shape, jnp.int32),
            pltpu.SMEM(token_mask.shape, jnp.int32),
            *[pltpu.VMEM(gain.shape, F32)] * 4,
            pltpu.VMEM(proj_in.shape[1:], BF),
            pltpu.VMEM(gate_in.shape[1:], BF),
            staged,
            pltpu.SemaphoreType.DMA((9,)),
        ],
        "project_first",
    )(*(
        pltpu.with_memory_space_constraint(x, pltpu.HBM)
        for x in (pairs, token_mask, mask_vec, gain, shift, out_gain, out_shift, proj_in, gate_in)
    ))

    def outgoing(other, made):
        (result,) = call(
            outgoing_kernel,
            [whole(sent_by_chip.shape), whole(own_columns)],
            [back_by_chip],
            [own_half, own_half, total],
            "outgoing",
        )(other, made[0])
        return result, made[1:]

    combined, (prior, gates, second_weights, column_vectors) = triangle(
        sent,
        call(
            outgoing_own_kernel,
            [
                whole(sent_by_chip.shape), whole(pairs.shape), whole(kept.shape), layer_of(gate_out, 0),
                layer_of(proj_in, 1), layer_of(gate_in, 1), whole(rows.shape),
            ],
            [shape(own_columns, F32), kept_wide, kept_wide, joined, columns],
            [own_half, own_half, total],
            "outgoing_own",
            flops,
        ),
        [pairs, normed, gate_out, proj_in, gate_in, vectors],
        outgoing,
    )
    sent, normed, first_pass = call(
        second_kernel,
        [
            whole(back.shape), whole(kept.shape), whole(kept.shape), whole(joined.shape),
            whole(columns.shape), whole(rows.shape), whole(rows.shape), layer_of(proj_out, 0),
        ],
        [send, kept, kept_wide],
        [staged, wide],
        "finish_and_project",
    )(combined, prior, gates, second_weights, column_vectors, weights, vectors, proj_out)

    def incoming(other, made):
        (result,) = call(
            incoming_kernel,
            [whole(sent_by_chip.shape), whole(own_columns), whole(own_columns)],
            [back_by_chip],
            [pltpu.VMEM(all_columns, BF)],
            "incoming",
        )(other, *made[:2])
        return result, made[2]

    combined, gates = triangle(
        sent,
        call(
            incoming_own_kernel,
            [whole(sent_by_chip.shape), whole(kept.shape), layer_of(gate_out, 1)],
            [shape(own_columns, BF), shape(own_columns, BF), kept_wide],
            [],
            "incoming_own",
            flops,
        ),
        [normed, gate_out],
        incoming,
    )
    (updated,) = call(
        third_kernel,
        [whole(back.shape), whole(kept.shape), whole(kept.shape), whole(columns.shape), layer_of(proj_out, 1)],
        [shape(pairs.shape, F32)],
        [wide],
        "finish",
    )(combined, first_pass, gates, column_vectors, proj_out)
    return updated.reshape(pair_field.shape)


def solution(mesh):
    rows, cols = mesh.devices.shape
    devices = np.asarray(mesh.devices).reshape(2, rows // 2, cols // 4, 2, 2)
    spec = P(("h", "x"), ("z", "y", "core"), None)
    return jax.shard_map(
        functools.partial(on_device, rows * cols // 2),
        mesh=Mesh(devices, ("h", "x", "z", "y", "core")),
        in_specs=(spec,) + (P(),) * 9,
        out_specs=spec,
        check_vma=False,
    )
```

profile of v0, /device:TPU:1, one launch (start us, length us, event | category | flops | bytes accessed | tf_op | source)
XLA Modules:
  0.0 105.5 jit_solution(7024538840335962719)
XLA Ops:
  0.0 2.2 %project_first.1 = (bf16[128,16,128]{2,1,0:T(8,128)(2,1)S(1)}, bf16[8,128,128]{2,1,0:T(8,128)(2,1)S(1)}, f32[8,128]{1,0:T(8,128)S(1)}, f32[8,128]{1,0:T(8,128)S(1)}) custom-call(f32[1024,128]{1,0:T(8,128)} %bitcast.9, s32[512]{0:T(512)} %mask_hbm.1, s32[4,128]{1,0:T(4,128)} %bitcast.17, f32[2,128]{1,0:T(2,128)} %gain_hbm.1, f32[2,128]{1,0:T(2,128)} %shift_hbm.1, ...), custom_call_target="tpu_custom_call" | custom-call | tf_op jit(solution)/shard_map/project_first/pallas_call | solution.py:318
  2.2 0.0 copy-start
  2.2 0.0 copy-start.1
  2.2 0.0 copy-start.2
  2.2 0.0 copy-start.4
  2.3 28.4 %all_to_all.20 = bf16[128,16,128]{2,1,0:T(8,128)(2,1)S(1)} all-to-all(bf16[128,16,128]{2,1,0:T(8,128)(2,1)S(1)} %get-tuple-element.40), channel_id=1, replica_groups={{216,248,152,184,88,120,24,56,218,250,154,186,90,122,26,58,200,232,136,..., dimensions={0} | all-to-all | bytes 1048576 | tf_op jit(solution)/shard_map/all_to_all | solution.py:307
  30.6 2.6 %collective-permute-start = (bf16[128,16,128]{2,1,0:T(8,128)(2,1)S(1)}, bf16[128,16,128]{2,1,0:T(8,128)(2,1)S(1)}, u32[]{:S(2)}, u32[]{:S(2)}) collective-permute-start(bf16[128,16,128]{2,1,0:T(8,128)(2,1)S(1)} %all_to_all.20), channel_id=1, source_target_pairs={{0,1},{1,0},{2,3},{3,2},{4,5},{5,4},{6,7},{7,6},{8,9},{9,8},{10,11... | collective-permute-start | bytes 1572872 | tf_op jit(solution)/shard_map/ppermute | solution.py:312
  33.2 0.0 copy-done
  33.2 0.0 copy-done.1
  33.2 0.0 copy-done.2
  33.2 0.0 copy-done.4
  33.2 1.1 %outgoing_own.1 = (f32[8,2,16,512]{3,2,1,0:T(8,128)S(1)}, f32[8,128,128]{2,1,0:T(8,128)S(1)}, f32[8,128,128]{2,1,0:T(8,128)S(1)}, bf16[512,128]{1,0:T(8,128)(2,1)S(1)}, f32[2,2,128,128]{3,2,1,0:T(8,128)S(1)}) custom-call(bf16[8,2,2,4,16,128]{5,4,3,2,1,0:T(8,128)(2,1)S(1)} %bitcast.11, f32[1024,128]{1,0:T(8,128)S(1)} %bitcast.10, ...), custom_call_target="tpu_custom_call" | custom-call | flops 33554432 | bytes 4194304 | tf_op jit(solution)/shard_map/outgoing_own/pallas_call | solution.py:313
  34.3 0.4 collective-permute-done
  34.7 0.8 outgoing.1
  35.5 0.0 copy-start.3
  35.5 19.1 %all_to_all.21.back_ref = bf16[128,8,128]{2,1,0:T(8,128)(2,1)S(1)} all-to-all(bf16[128,8,128]{2,1,0:T(8,128)(2,1)S(1)} %bitcast.14), channel_id=1, replica_groups={{216,248,152,184,88,120,24,56,218,250,154,186,90,122,26,58,200,232,136,..., dimensions={0} | all-to-all | bytes 524288 | tf_op jit(solution)/shard_map/all_to_all | solution.py:307
  54.7 0.0 copy-done.3
  54.7 1.6 %finish_and_project.1 = (bf16[128,16,128]{2,1,0:T(8,128)(2,1)S(1)}, bf16[8,128,128]{2,1,0:T(8,128)(2,1)S(1)}, f32[8,128,128]{2,1,0:T(8,128)S(1)}) custom-call(bf16[128,8,128]{2,1,0:T(8,128)(2,1)S(1)} %all_to_all.21.back_ref, f32[8,128,128]{2,1,0:T(8,128)S(1)} %get-tuple-element.57.prior_ref, f32[8,128,128]{2,1,0:T(8,128)S(1)} %get-tuple-element.58.gates_ref, ...), custom_call_target="tpu_custom_call" | custom-call | tf_op jit(solution)/shard_map/finish_and_project/pallas_call | solution.py:364
  56.3 23.0 %all_to_all.22 = bf16[128,16,128]{2,1,0:T(8,128)(2,1)S(1)} all-to-all(bf16[128,16,128]{2,1,0:T(8,128)(2,1)S(1)} %get-tuple-element.62), channel_id=1, replica_groups={{216,248,152,184,88,120,24,56,218,250,154,186,90,122,26,58,200,232,136,..., dimensions={0} | all-to-all | bytes 1048576 | tf_op jit(solution)/shard_map/all_to_all | solution.py:307
  79.4 3.7 %collective-permute-start.1 = (bf16[128,16,128]{2,1,0:T(8,128)(2,1)S(1)}, bf16[128,16,128]{2,1,0:T(8,128)(2,1)S(1)}, u32[]{:S(2)}, u32[]{:S(2)}) collective-permute-start(bf16[128,16,128]{2,1,0:T(8,128)(2,1)S(1)} %all_to_all.22), channel_id=1, source_target_pairs={{0,1},{1,0},{2,3},{3,2},{4,5},{5,4},{6,7},{7,6},{8,9},{9,8},{10,11... | collective-permute-start | bytes 1572872 | tf_op jit(solution)/shard_map/ppermute | solution.py:312
  83.1 0.3 incoming_own.1
  83.4 1.2 %collective-permute-done.1 = bf16[128,16,128]{2,1,0:T(8,128)(2,1)S(1)} collective-permute-done((bf16[128,16,128]{2,1,0:T(8,128)(2,1)S(1)}, bf16[128,16,128]{2,1,0:T(8,128)(2,1)S(1)}, u32[]{:S(2)}, u32[]{:S(2)}) %collective-permute-start.1) | collective-permute-done | bytes 524320 | tf_op jit(solution)/shard_map/ppermute | solution.py:312
  84.6 0.5 incoming.1
  85.1 19.0 %all_to_all.23.back_ref = bf16[128,8,128]{2,1,0:T(8,128)(2,1)S(1)} all-to-all(bf16[128,8,128]{2,1,0:T(8,128)(2,1)S(1)} %bitcast.13), channel_id=1, replica_groups={{216,248,152,184,88,120,24,56,218,250,154,186,90,122,26,58,200,232,136,..., dimensions={0} | all-to-all | bytes 524288 | tf_op jit(solution)/shard_map/all_to_all | solution.py:307
  104.1 1.4 %finish.1 = f32[1024,128]{1,0:T(8,128)} custom-call(bf16[128,8,128]{2,1,0:T(8,128)(2,1)S(1)} %all_to_all.23.back_ref, f32[8,128,128]{2,1,0:T(8,128)S(1)} %get-tuple-element.73.pass_ref, f32[8,128,128]{2,1,0:T(8,128)S(1)} %get-tuple-element.74.gates_ref, f32[2,2,128,128]{3,2,1,0:T(8,128)S(1)} %get-tuple-element.60.columns_ref, bf16[2,128,128]{2,1,0:T(8,128)(2,1)S(1)} %copy-done.3), custom_call_target="tpu_custom_call" | custom-call | tf_op jit(solution)/shard_map/finish/pallas_call | solution.py:398
Async XLA Ops:
  2.2 31.0 %copy-start = (f32[64,16,128]{2,1,0:T(8,128)S(1)}, f32[64,16,128]{2,1,0:T(8,128)}, u32[]{:S(2)}) copy-start(f32[64,16,128]{2,1,0:T(8,128)} %param.10) | copy-start | bytes 1572868
  2.2 31.0 %copy-start.1 = (bf16[2,128,256]{2,1,0:T(8,128)(2,1)S(1)}, bf16[2,128,256]{2,1,0:T(8,128)(2,1)}, u32[]{:S(2)}) copy-start(bf16[2,128,256]{2,1,0:T(8,128)(2,1)} %proj_in) | copy-start | bytes 393220
  2.2 31.0 %copy-start.2 = (bf16[2,128,256]{2,1,0:T(8,128)(2,1)S(1)}, bf16[2,128,256]{2,1,0:T(8,128)(2,1)}, u32[]{:S(2)}) copy-start(bf16[2,128,256]{2,1,0:T(8,128)(2,1)} %gate_in) | copy-start | bytes 393220
  2.2 31.0 %copy-start.4 = (bf16[2,128,128]{2,1,0:T(8,128)(2,1)S(1)}, bf16[2,128,128]{2,1,0:T(8,128)(2,1)}, u32[]{:S(2)}) copy-start(bf16[2,128,128]{2,1,0:T(8,128)(2,1)} %gate_out.1) | copy-start | bytes 196612
  30.6 4.1 %collective-permute-start = (bf16[128,16,128]{2,1,0:T(8,128)(2,1)S(1)}, bf16[128,16,128]{2,1,0:T(8,128)(2,1)S(1)}, u32[]{:S(2)}, u32[]{:S(2)}) collective-permute-start(bf16[128,16,128]{2,1,0:T(8,128)(2,1)S(1)} %all_to_all.20), channel_id=1, source_target_pairs={{0,1},{1,0},{2,3},{3,2},{4,5},{5,4},{6,7},{7,6},{8,9},{9,8},{10,11... | collective-permute-start | bytes 1572872 | tf_op jit(solution)/shard_map/ppermute | solution.py:312
  35.5 19.2 %copy-start.3 = (bf16[2,128,128]{2,1,0:T(8,128)(2,1)S(1)}, bf16[2,128,128]{2,1,0:T(8,128)(2,1)}, u32[]{:S(2)}) copy-start(bf16[2,128,128]{2,1,0:T(8,128)(2,1)} %proj_out.3) | copy-start | bytes 196612
  79.4 5.2 %collective-permute-start.1 = (bf16[128,16,128]{2,1,0:T(8,128)(2,1)S(1)}, bf16[128,16,128]{2,1,0:T(8,128)(2,1)S(1)}, u32[]{:S(2)}, u32[]{:S(2)}) collective-permute-start(bf16[128,16,128]{2,1,0:T(8,128)(2,1)S(1)} %all_to_all.22), channel_id=1, source_target_pairs={{0,1},{1,0},{2,3},{3,2},{4,5},{5,4},{6,7},{7,6},{8,9},{9,8},{10,11... | collective-permute-start | bytes 1572872 | tf_op jit(solution)/shard_map/ppermute | solution.py:312
where the time goes:
time: 106 us; the launch traced here: 105 us
  blocking collectives  89.5 us (84%)
  Pallas kernels  7.91 us (7%)
  starting transfers between devices  6.26 us (6%)
  waiting for transfers between devices  1.64 us (2%)
    all_to_all x4, blocking collectives, exchange(): return lax.all_to_all(x, axes, 0, 0, axis_index_groups=groups, tiled=True)  89.5 us
    ppermute x2, starting transfers between devices, triangle(): other = lax.ppermute(mine, 'core', [(0, 1), (1, 0)])  6.26 us
    pallas_call x1, Pallas kernels, on_device(): call(first_kernel, [HBM] * 9, [send, kept, rows, rows], [pltpu.VMEM(pairs...  2.2 us
  transfers between devices with their start and end apart: 2, of which 2 were waited for; matrix products, arithmetic and copies ran while one was open for 0% of the time, Pallas kernels for 1%

commit v1 on v0

--- a/solution.py
+++ b/solution.py
@@ -13,7 +13,7 @@
 ROWS, LANES, HALF = 8, 128, 64
 BF, F32 = jnp.bfloat16, jnp.float32
 VMEM_LIMIT = 40 * 1024 * 1024
-ORDER = ("z", "y", "h", "x")
+ORDER = ("z", "h", "x", "y")
 LISTS = {"z": (6, 2, 7, 3, 0, 4, 1, 5), "y": (0, 1), "h": (1, 0), "x": (2, 3, 0, 1)}
 
 
@@ -223,20 +223,19 @@
     scatter_rows(partial_ref[...] + outgoing_product(other_ref, left, right, total), out_ref)
 
 
-def incoming_own_kernel(own_ref, normed_ref, gate_out, left_ref, right_ref, gates_ref):
+def incoming_left_kernel(own_ref, left_ref):
     gather_rows(own_ref, 0, keep_in(left_ref))
+
+
+def incoming_right_kernel(own_ref, normed_ref, gate_out, right_ref, gates_ref):
     gather_rows(own_ref, 1, keep_in(right_ref))
     gates_of(normed_ref, gate_out, gates_ref)
 
 
-def incoming_kernel(other_ref, left_ref, right_ref, out_ref, left):
+def incoming_kernel(left_ref, other_ref, right_ref, out_ref, left):
     core = lax.axis_index("core")
     left[:, :, core] = left_ref[...]
-
-    def store(lanes, tile):
-        left[:, :, 1 - core, :, lanes] = tile
-
-    gather_rows(other_ref, 0, store)
+    left[:, :, 1 - core] = other_ref[...]
     tokens = left.shape[-1]
     lefts, rights = left[...].reshape(-1, tokens), right_ref[...].reshape(-1, tokens)
     product = lax.dot_general(rights, lefts, (((1,), (1,)), ((), ())), preferred_element_type=F32)
@@ -306,14 +305,8 @@
     def exchange(x):
         return lax.all_to_all(x, axes, 0, 0, axis_index_groups=groups, tiled=True)
 
-    def triangle(sent, own_call, own_operands, other_call):
-        mine = exchange(sent)
-        mine, *own_operands = lax.optimization_barrier([mine, *own_operands])
-        other = lax.ppermute(mine, "core", [(0, 1), (1, 0)])
-        made = own_call(mine.reshape(sent_by_chip.shape), *own_operands)
-        other, made = lax.optimization_barrier((other, made))
-        result, aside = other_call(other.reshape(sent_by_chip.shape), made)
-        return exchange(result.reshape(back.shape)), aside
+    def swap_cores(x):
+        return lax.ppermute(x, "core", [(0, 1), (1, 0)])
 
     sent, normed, weights, vectors = call(
         first_kernel,
@@ -335,32 +328,28 @@
         for x in (pairs, token_mask, mask_vec, gain, shift, out_gain, out_shift, proj_in, gate_in)
     ))
 
-    def outgoing(other, made):
-        (result,) = call(
-            outgoing_kernel,
-            [whole(sent_by_chip.shape), whole(own_columns)],
-            [back_by_chip],
-            [own_half, own_half, total],
-            "outgoing",
-        )(other, made[0])
-        return result, made[1:]
-
-    combined, (prior, gates, second_weights, column_vectors) = triangle(
-        sent,
-        call(
-            outgoing_own_kernel,
-            [
-                whole(sent_by_chip.shape), whole(pairs.shape), whole(kept.shape), layer_of(gate_out, 0),
-                layer_of(proj_in, 1), layer_of(gate_in, 1), whole(rows.shape),
-            ],
-            [shape(own_columns, F32), kept_wide, kept_wide, joined, columns],
-            [own_half, own_half, total],
-            "outgoing_own",
-            flops,
-        ),
-        [pairs, normed, gate_out, proj_in, gate_in, vectors],
-        outgoing,
-    )
+    mine, pairs, normed = lax.optimization_barrier((exchange(sent), pairs, normed))
+    other = swap_cores(mine)
+    made = call(
+        outgoing_own_kernel,
+        [
+            whole(sent_by_chip.shape), whole(pairs.shape), whole(kept.shape), layer_of(gate_out, 0),
+            layer_of(proj_in, 1), layer_of(gate_in, 1), whole(rows.shape),
+        ],
+        [shape(own_columns, F32), kept_wide, kept_wide, joined, columns],
+        [own_half, own_half, total],
+        "outgoing_own",
+        flops,
+    )(mine.reshape(sent_by_chip.shape), pairs, normed, gate_out, proj_in, gate_in, vectors)
+    other, (partial, prior, gates, second_weights, column_vectors) = lax.optimization_barrier((other, made))
+    (result,) = call(
+        outgoing_kernel,
+        [whole(sent_by_chip.shape), whole(own_columns)],
+        [back_by_chip],
+        [own_half, own_half, total],
+        "outgoing",
+    )(other.reshape(sent_by_chip.shape), partial)
+    combined = exchange(result.reshape(back.shape))
     sent, normed, first_pass = call(
         second_kernel,
         [
@@ -372,29 +361,33 @@
         "finish_and_project",
     )(combined, prior, gates, second_weights, column_vectors, weights, vectors, proj_out)
 
-    def incoming(other, made):
-        (result,) = call(
-            incoming_kernel,
-            [whole(sent_by_chip.shape), whole(own_columns), whole(own_columns)],
-            [back_by_chip],
-            [pltpu.VMEM(all_columns, BF)],
-            "incoming",
-        )(other, *made[:2])
-        return result, made[2]
-
-    combined, gates = triangle(
-        sent,
-        call(
-            incoming_own_kernel,
-            [whole(sent_by_chip.shape), whole(kept.shape), layer_of(gate_out, 1)],
-            [shape(own_columns, BF), shape(own_columns, BF), kept_wide],
-            [],
-            "incoming_own",
-            flops,
-        ),
-        [normed, gate_out],
-        incoming,
-    )
+    mine, normed = lax.optimization_barrier((exchange(sent).reshape(sent_by_chip.shape), normed))
+    (left,) = call(
+        incoming_left_kernel,
+        [whole(sent_by_chip.shape)],
+        [shape(own_columns, BF)],
+        [],
+        "incoming_left",
+    )(mine)
+    mine, left, normed = lax.optimization_barrier((mine, left, normed))
+    other = swap_cores(left)
+    made = call(
+        incoming_right_kernel,
+        [whole(sent_by_chip.shape), whole(kept.shape), layer_of(gate_out, 1)],
+        [shape(own_columns, BF), kept_wide],
+        [],
+        "incoming_right",
+        flops,
+    )(mine, normed, gate_out)
+    other, (right, gates) = lax.optimization_barrier((other, made))
+    (result,) = call(
+        incoming_kernel,
+        [whole(own_columns)] * 3,
+        [back_by_chip],
+        [pltpu.VMEM(all_columns, BF)],
+        "incoming",
+    )(left, other, right)
+    combined = exchange(result.reshape(back.shape))
     (updated,) = call(
         third_kernel,
         [whole(back.shape), whole(kept.shape), whole(kept.shape), whole(columns.shape), layer_of(proj_out, 1)],

time: 106 us -> 105 us (level)
    pallas_call x4 -> x5, Pallas kernels: 2.71 us -> 2.66 us  [the longest x1 1.05 us: on_device(): call(outgoing_own_kernel, [whole(sent_by_chip.shape), whole(pairs.shape),...]
where the time goes in v1:
time: 105 us; the launch traced here: 104 us
  blocking collectives  88.9 us (85%)
  Pallas kernels  7.83 us (7%)
  starting transfers between devices  6.29 us (6%)
  waiting for transfers between devices  1.36 us (1%)
    all_to_all x4, blocking collectives, exchange(): return lax.all_to_all(x, axes, 0, 0, axis_index_groups=groups, tiled=True)  88.9 us
    ppermute x2, starting transfers between devices, swap_cores(): return lax.ppermute(x, 'core', [(0, 1), (1, 0)])  6.29 us
    pallas_call x1, Pallas kernels, on_device(): call(first_kernel, [HBM] * 9, [send, kept, rows, rows], [pltpu.VMEM(pairs...  2.2 us
  transfers between devices with their start and end apart: 2, of which 2 were waited for; matrix products, arithmetic and copies ran while one was open for 0% of the time, Pallas kernels for 1%

profile of v1, /device:TPU:1, one launch (start us, length us, event | category | flops | bytes accessed | tf_op | source)
XLA Modules:
  0.0 104.5 jit_solution(8616073233420747596)
XLA Ops:
  0.0 2.2 %project_first.1 = (bf16[128,16,128]{2,1,0:T(8,128)(2,1)S(1)}, bf16[8,128,128]{2,1,0:T(8,128)(2,1)S(1)}, f32[8,128]{1,0:T(8,128)S(1)}, f32[8,128]{1,0:T(8,128)S(1)}) custom-call(f32[1024,128]{1,0:T(8,128)} %bitcast.10, s32[512]{0:T(512)} %mask_hbm.1, s32[4,128]{1,0:T(4,128)} %bitcast.16, f32[2,128]{1,0:T(2,128)} %gain_hbm.1, f32[2,128]{1,0:T(2,128)} %shift_hbm.1, ...), custom_call_target="tpu_custom_call" | custom-call | tf_op jit(solution)/shard_map/project_first/pallas_call | solution.py:311
  2.2 0.0 copy-start
  2.2 0.0 copy-start.1
  2.2 0.0 copy-start.2
  2.2 0.0 copy-start.4
  2.3 28.2 %all_to_all.20 = bf16[128,16,128]{2,1,0:T(8,128)(2,1)S(1)} all-to-all(bf16[128,16,128]{2,1,0:T(8,128)(2,1)S(1)} %get-tuple-element.36), channel_id=1, replica_groups={{216,218,248,250,152,154,184,186,88,90,120,122,24,26,56,58,200,202,232,..., dimensions={0} | all-to-all | bytes 1048576 | tf_op jit(solution)/shard_map/all_to_all | solution.py:306
  30.5 2.8 %collective-permute-start = (bf16[128,16,128]{2,1,0:T(8,128)(2,1)S(1)}, bf16[128,16,128]{2,1,0:T(8,128)(2,1)S(1)}, u32[]{:S(2)}, u32[]{:S(2)}) collective-permute-start(bf16[128,16,128]{2,1,0:T(8,128)(2,1)S(1)} %all_to_all.20), channel_id=1, source_target_pairs={{0,1},{1,0},{2,3},{3,2},{4,5},{5,4},{6,7},{7,6},{8,9},{9,8},{10,11... | collective-permute-start | bytes 1572872 | tf_op jit(solution)/shard_map/ppermute | solution.py:309
  33.3 0.0 copy-done
  33.3 0.0 copy-done.1
  33.3 0.0 copy-done.2
  33.3 0.0 copy-done.4
  33.3 1.0 %outgoing_own.1 = (f32[8,2,16,512]{3,2,1,0:T(8,128)S(1)}, f32[8,128,128]{2,1,0:T(8,128)S(1)}, f32[8,128,128]{2,1,0:T(8,128)S(1)}, bf16[512,128]{1,0:T(8,128)(2,1)S(1)}, f32[2,2,128,128]{3,2,1,0:T(8,128)S(1)}) custom-call(bf16[8,2,4,2,16,128]{5,4,3,2,1,0:T(8,128)(2,1)S(1)} %bitcast.12, f32[1024,128]{1,0:T(8,128)S(1)} %bitcast.11, ...), custom_call_target="tpu_custom_call" | custom-call | flops 33554432 | bytes 4194304 | tf_op jit(solution)/shard_map/outgoing_own/pallas_call | solution.py:333
  34.3 0.5 collective-permute-done
  34.8 0.8 outgoing.1
  35.6 0.0 copy-start.3
  35.6 18.5 %all_to_all.21.back_ref = bf16[128,8,128]{2,1,0:T(8,128)(2,1)S(1)} all-to-all(bf16[128,8,128]{2,1,0:T(8,128)(2,1)S(1)} %bitcast.13), channel_id=1, replica_groups={{216,218,248,250,152,154,184,186,88,90,120,122,24,26,56,58,200,202,232,..., dimensions={0} | all-to-all | bytes 524288 | tf_op jit(solution)/shard_map/all_to_all | solution.py:306
  54.1 0.0 copy-done.3
  54.1 1.6 %finish_and_project.1 = (bf16[128,16,128]{2,1,0:T(8,128)(2,1)S(1)}, bf16[8,128,128]{2,1,0:T(8,128)(2,1)S(1)}, f32[8,128,128]{2,1,0:T(8,128)S(1)}) custom-call(bf16[128,8,128]{2,1,0:T(8,128)(2,1)S(1)} %all_to_all.21.back_ref, f32[8,128,128]{2,1,0:T(8,128)S(1)} %get-tuple-element.49.prior_ref, f32[8,128,128]{2,1,0:T(8,128)S(1)} %get-tuple-element.50.gates_ref, ...), custom_call_target="tpu_custom_call" | custom-call | tf_op jit(solution)/shard_map/finish_and_project/pallas_call | solution.py:353
  55.7 23.8 %all_to_all.22 = bf16[128,16,128]{2,1,0:T(8,128)(2,1)S(1)} all-to-all(bf16[128,16,128]{2,1,0:T(8,128)(2,1)S(1)} %get-tuple-element.54), channel_id=1, replica_groups={{216,218,248,250,152,154,184,186,88,90,120,122,24,26,56,58,200,202,232,..., dimensions={0} | all-to-all | bytes 1048576 | tf_op jit(solution)/shard_map/all_to_all | solution.py:306
  79.5 0.1 incoming_left.1.left_ref
  79.7 3.5 %collective-permute-start.1 = (bf16[8,2,16,512]{3,2,1,0:T(8,128)(2,1)S(1)}, bf16[8,2,16,512]{3,2,1,0:T(8,128)(2,1)S(1)}, u32[]{:S(2)}, u32[]{:S(2)}) collective-permute-start(bf16[8,2,16,512]{3,2,1,0:T(8,128)(2,1)S(1)} %incoming_left.1.left_ref), channel_id=1, source_target_pairs={{0,1},{1,0},{2,3},{3,2},{4,5},{5,4},{6,7},{7,6},{8,9},{9,8},{10,11... | collective-permute-start | bytes 786440 | tf_op jit(solution)/shard_map/ppermute | solution.py:309
  83.2 0.3 incoming_right.1
  83.5 0.9 collective-permute-done.1.other_ref
  84.3 0.4 incoming.1
  84.8 18.3 %all_to_all.23.back_ref = bf16[128,8,128]{2,1,0:T(8,128)(2,1)S(1)} all-to-all(bf16[128,8,128]{2,1,0:T(8,128)(2,1)S(1)} %bitcast.14), channel_id=1, replica_groups={{216,218,248,250,152,154,184,186,88,90,120,122,24,26,56,58,200,202,232,..., dimensions={0} | all-to-all | bytes 524288 | tf_op jit(solution)/shard_map/all_to_all | solution.py:306
  103.1 1.3 %finish.1 = f32[1024,128]{1,0:T(8,128)} custom-call(bf16[128,8,128]{2,1,0:T(8,128)(2,1)S(1)} %all_to_all.23.back_ref, f32[8,128,128]{2,1,0:T(8,128)S(1)} %get-tuple-element.65.pass_ref, f32[8,128,128]{2,1,0:T(8,128)S(1)} %get-tuple-element.66.gates_ref, f32[2,2,128,128]{3,2,1,0:T(8,128)S(1)} %get-tuple-element.52.columns_ref, bf16[2,128,128]{2,1,0:T(8,128)(2,1)S(1)} %copy-done.3), custom_call_target="tpu_custom_call" | custom-call | tf_op jit(solution)/shard_map/finish/pallas_call | solution.py:391
Async XLA Ops:
  2.2 31.1 %copy-start = (f32[64,16,128]{2,1,0:T(8,128)S(1)}, f32[64,16,128]{2,1,0:T(8,128)}, u32[]{:S(2)}) copy-start(f32[64,16,128]{2,1,0:T(8,128)} %param.10) | copy-start | bytes 1572868
  2.2 31.1 %copy-start.1 = (bf16[2,128,256]{2,1,0:T(8,128)(2,1)S(1)}, bf16[2,128,256]{2,1,0:T(8,128)(2,1)}, u32[]{:S(2)}) copy-start(bf16[2,128,256]{2,1,0:T(8,128)(2,1)} %proj_in.1) | copy-start | bytes 393220
  2.2 31.1 %copy-start.2 = (bf16[2,128,256]{2,1,0:T(8,128)(2,1)S(1)}, bf16[2,128,256]{2,1,0:T(8,128)(2,1)}, u32[]{:S(2)}) copy-start(bf16[2,128,256]{2,1,0:T(8,128)(2,1)} %gate_in.1) | copy-start | bytes 393220
  2.2 31.0 %copy-start.4 = (bf16[2,128,128]{2,1,0:T(8,128)(2,1)S(1)}, bf16[2,128,128]{2,1,0:T(8,128)(2,1)}, u32[]{:S(2)}) copy-start(bf16[2,128,128]{2,1,0:T(8,128)(2,1)} %gate_out.3) | copy-start | bytes 196612
  30.5 4.3 %collective-permute-start = (bf16[128,16,128]{2,1,0:T(8,128)(2,1)S(1)}, bf16[128,16,128]{2,1,0:T(8,128)(2,1)S(1)}, u32[]{:S(2)}, u32[]{:S(2)}) collective-permute-start(bf16[128,16,128]{2,1,0:T(8,128)(2,1)S(1)} %all_to_all.20), channel_id=1, source_target_pairs={{0,1},{1,0},{2,3},{3,2},{4,5},{5,4},{6,7},{7,6},{8,9},{9,8},{10,11... | collective-permute-start | bytes 1572872 | tf_op jit(solution)/shard_map/ppermute | solution.py:309
  35.6 18.5 %copy-start.3 = (bf16[2,128,128]{2,1,0:T(8,128)(2,1)S(1)}, bf16[2,128,128]{2,1,0:T(8,128)(2,1)}, u32[]{:S(2)}) copy-start(bf16[2,128,128]{2,1,0:T(8,128)(2,1)} %proj_out.3) | copy-start | bytes 196612
  79.7 4.7 %collective-permute-start.1 = (bf16[8,2,16,512]{3,2,1,0:T(8,128)(2,1)S(1)}, bf16[8,2,16,512]{3,2,1,0:T(8,128)(2,1)S(1)}, u32[]{:S(2)}, u32[]{:S(2)}) collective-permute-start(bf16[8,2,16,512]{3,2,1,0:T(8,128)(2,1)S(1)} %incoming_left.1.left_ref), channel_id=1, source_target_pairs={{0,1},{1,0},{2,3},{3,2},{4,5},{5,4},{6,7},{7,6},{8,9},{9,8},{10,11... | collective-permute-start | bytes 786440 | tf_op jit(solution)/shard_map/ppermute | solution.py:309

commit v2 on v1

--- a/solution.py
+++ b/solution.py
@@ -14,7 +14,7 @@
 BF, F32 = jnp.bfloat16, jnp.float32
 VMEM_LIMIT = 40 * 1024 * 1024
 ORDER = ("z", "h", "x", "y")
-LISTS = {"z": (6, 2, 7, 3, 0, 4, 1, 5), "y": (0, 1), "h": (1, 0), "x": (2, 3, 0, 1)}
+LISTS = {"z": (5, 1, 6, 2, 7, 3, 0, 4), "y": (0, 1), "h": (1, 0), "x": (2, 3, 0, 1)}
 
 
 def sigmoid(x):

time: 105 us -> 105 us (level)
  no operation moved by 1% of the time
where the time goes in v2:
time: 105 us
  blocking collectives  89.8 us (86%)
  Pallas kernels  7.82 us (7%)
  starting transfers between devices  5.44 us (5%)
  waiting for transfers between devices  1.36 us (1%)
    all_to_all x4, blocking collectives, exchange(): return lax.all_to_all(x, axes, 0, 0, axis_index_groups=groups, tiled=True)  89.8 us
    ppermute x2, starting transfers between devices, swap_cores(): return lax.ppermute(x, 'core', [(0, 1), (1, 0)])  5.44 us
    pallas_call x1, Pallas kernels, on_device(): call(first_kernel, [HBM] * 9, [send, kept, rows, rows], [pltpu.VMEM(pairs...  2.2 us
  transfers between devices with their start and end apart: 2, of which 2 were waited for; matrix products, arithmetic and copies ran while one was open for 0% of the time, Pallas kernels for 1%

profile of v2, /device:TPU:1, one launch (start us, length us, event | category | flops | bytes accessed | tf_op | source)
XLA Modules:
  0.0 104.5 jit_solution(9363427698582924703)
XLA Ops:
  0.0 2.2 %project_first.1 = (bf16[128,16,128]{2,1,0:T(8,128)(2,1)S(1)}, bf16[8,128,128]{2,1,0:T(8,128)(2,1)S(1)}, f32[8,128]{1,0:T(8,128)S(1)}, f32[8,128]{1,0:T(8,128)S(1)}) custom-call(f32[1024,128]{1,0:T(8,128)} %bitcast.10, s32[512]{0:T(512)} %mask_hbm.1, s32[4,128]{1,0:T(4,128)} %bitcast.16, f32[2,128]{1,0:T(2,128)} %gain_hbm.1, f32[2,128]{1,0:T(2,128)} %shift_hbm.1, ...), custom_call_target="tpu_custom_call" | custom-call | tf_op jit(solution)/shard_map/project_first/pallas_call | solution.py:311
  2.2 0.0 copy-start
  2.2 0.0 copy-start.1
  2.2 0.0 copy-start.2
  2.2 0.0 copy-start.4
  2.3 28.8 %all_to_all.20 = bf16[128,16,128]{2,1,0:T(8,128)(2,1)S(1)} all-to-all(bf16[128,16,128]{2,1,0:T(8,128)(2,1)S(1)} %get-tuple-element.36), channel_id=1, replica_groups={{212,214,244,246,148,150,180,182,84,86,116,118,20,22,52,54,196,198,228,..., dimensions={0} | all-to-all | bytes 1048576 | tf_op jit(solution)/shard_map/all_to_all | solution.py:306
  31.0 2.1 %collective-permute-start = (bf16[128,16,128]{2,1,0:T(8,128)(2,1)S(1)}, bf16[128,16,128]{2,1,0:T(8,128)(2,1)S(1)}, u32[]{:S(2)}, u32[]{:S(2)}) collective-permute-start(bf16[128,16,128]{2,1,0:T(8,128)(2,1)S(1)} %all_to_all.20), channel_id=1, source_target_pairs={{0,1},{1,0},{2,3},{3,2},{4,5},{5,4},{6,7},{7,6},{8,9},{9,8},{10,11... | collective-permute-start | bytes 1572872 | tf_op jit(solution)/shard_map/ppermute | solution.py:309
  33.2 0.0 copy-done
  33.2 0.0 copy-done.1
  33.2 0.0 copy-done.2
  33.2 0.0 copy-done.4
  33.2 1.0 outgoing_own.1
  34.2 0.5 collective-permute-done
  34.7 0.8 outgoing.1
  35.4 0.0 copy-start.3
  35.5 19.2 %all_to_all.21.back_ref = bf16[128,8,128]{2,1,0:T(8,128)(2,1)S(1)} all-to-all(bf16[128,8,128]{2,1,0:T(8,128)(2,1)S(1)} %bitcast.13), channel_id=1, replica_groups={{212,214,244,246,148,150,180,182,84,86,116,118,20,22,52,54,196,198,228,..., dimensions={0} | all-to-all | bytes 524288 | tf_op jit(solution)/shard_map/all_to_all | solution.py:306
  54.6 0.0 copy-done.3
  54.6 1.6 %finish_and_project.1 = (bf16[128,16,128]{2,1,0:T(8,128)(2,1)S(1)}, bf16[8,128,128]{2,1,0:T(8,128)(2,1)S(1)}, f32[8,128,128]{2,1,0:T(8,128)S(1)}) custom-call(bf16[128,8,128]{2,1,0:T(8,128)(2,1)S(1)} %all_to_all.21.back_ref, f32[8,128,128]{2,1,0:T(8,128)S(1)} %get-tuple-element.49.prior_ref, f32[8,128,128]{2,1,0:T(8,128)S(1)} %get-tuple-element.50.gates_ref, ...), custom_call_target="tpu_custom_call" | custom-call | tf_op jit(solution)/shard_map/finish_and_project/pallas_call | solution.py:353
  56.3 22.7 %all_to_all.22 = bf16[128,16,128]{2,1,0:T(8,128)(2,1)S(1)} all-to-all(bf16[128,16,128]{2,1,0:T(8,128)(2,1)S(1)} %get-tuple-element.54), channel_id=1, replica_groups={{212,214,244,246,148,150,180,182,84,86,116,118,20,22,52,54,196,198,228,..., dimensions={0} | all-to-all | bytes 1048576 | tf_op jit(solution)/shard_map/all_to_all | solution.py:306
  79.0 0.1 incoming_left.1.left_ref
  79.2 3.3 %collective-permute-start.1 = (bf16[8,2,16,512]{3,2,1,0:T(8,128)(2,1)S(1)}, bf16[8,2,16,512]{3,2,1,0:T(8,128)(2,1)S(1)}, u32[]{:S(2)}, u32[]{:S(2)}) collective-permute-start(bf16[8,2,16,512]{3,2,1,0:T(8,128)(2,1)S(1)} %incoming_left.1.left_ref), channel_id=1, source_target_pairs={{0,1},{1,0},{2,3},{3,2},{4,5},{5,4},{6,7},{7,6},{8,9},{9,8},{10,11... | collective-permute-start | bytes 786440 | tf_op jit(solution)/shard_map/ppermute | solution.py:309
  82.5 0.3 incoming_right.1
  82.8 0.9 collective-permute-done.1.other_ref
  83.7 0.4 incoming.1
  84.1 19.1 %all_to_all.23.back_ref = bf16[128,8,128]{2,1,0:T(8,128)(2,1)S(1)} all-to-all(bf16[128,8,128]{2,1,0:T(8,128)(2,1)S(1)} %bitcast.14), channel_id=1, replica_groups={{212,214,244,246,148,150,180,182,84,86,116,118,20,22,52,54,196,198,228,..., dimensions={0} | all-to-all | bytes 524288 | tf_op jit(solution)/shard_map/all_to_all | solution.py:306
  103.2 1.3 %finish.1 = f32[1024,128]{1,0:T(8,128)} custom-call(bf16[128,8,128]{2,1,0:T(8,128)(2,1)S(1)} %all_to_all.23.back_ref, f32[8,128,128]{2,1,0:T(8,128)S(1)} %get-tuple-element.65.pass_ref, f32[8,128,128]{2,1,0:T(8,128)S(1)} %get-tuple-element.66.gates_ref, f32[2,2,128,128]{3,2,1,0:T(8,128)S(1)} %get-tuple-element.52.columns_ref, bf16[2,128,128]{2,1,0:T(8,128)(2,1)S(1)} %copy-done.3), custom_call_target="tpu_custom_call" | custom-call | tf_op jit(solution)/shard_map/finish/pallas_call | solution.py:391
Async XLA Ops:
  2.2 30.9 %copy-start = (f32[64,16,128]{2,1,0:T(8,128)S(1)}, f32[64,16,128]{2,1,0:T(8,128)}, u32[]{:S(2)}) copy-start(f32[64,16,128]{2,1,0:T(8,128)} %param.10) | copy-start | bytes 1572868
  2.2 30.9 %copy-start.1 = (bf16[2,128,256]{2,1,0:T(8,128)(2,1)S(1)}, bf16[2,128,256]{2,1,0:T(8,128)(2,1)}, u32[]{:S(2)}) copy-start(bf16[2,128,256]{2,1,0:T(8,128)(2,1)} %proj_in.1) | copy-start | bytes 393220
  2.2 30.9 %copy-start.2 = (bf16[2,128,256]{2,1,0:T(8,128)(2,1)S(1)}, bf16[2,128,256]{2,1,0:T(8,128)(2,1)}, u32[]{:S(2)}) copy-start(bf16[2,128,256]{2,1,0:T(8,128)(2,1)} %gate_in.1) | copy-start | bytes 393220
  2.2 30.9 %copy-start.4 = (bf16[2,128,128]{2,1,0:T(8,128)(2,1)S(1)}, bf16[2,128,128]{2,1,0:T(8,128)(2,1)}, u32[]{:S(2)}) copy-start(bf16[2,128,128]{2,1,0:T(8,128)(2,1)} %gate_out.3) | copy-start | bytes 196612
  31.0 3.6 %collective-permute-start = (bf16[128,16,128]{2,1,0:T(8,128)(2,1)S(1)}, bf16[128,16,128]{2,1,0:T(8,128)(2,1)S(1)}, u32[]{:S(2)}, u32[]{:S(2)}) collective-permute-start(bf16[128,16,128]{2,1,0:T(8,128)(2,1)S(1)} %all_to_all.20), channel_id=1, source_target_pairs={{0,1},{1,0},{2,3},{3,2},{4,5},{5,4},{6,7},{7,6},{8,9},{9,8},{10,11... | collective-permute-start | bytes 1572872 | tf_op jit(solution)/shard_map/ppermute | solution.py:309
  35.4 19.2 %copy-start.3 = (bf16[2,128,128]{2,1,0:T(8,128)(2,1)S(1)}, bf16[2,128,128]{2,1,0:T(8,128)(2,1)}, u32[]{:S(2)}) copy-start(bf16[2,128,128]{2,1,0:T(8,128)(2,1)} %proj_out.3) | copy-start | bytes 196612
  79.2 4.5 %collective-permute-start.1 = (bf16[8,2,16,512]{3,2,1,0:T(8,128)(2,1)S(1)}, bf16[8,2,16,512]{3,2,1,0:T(8,128)(2,1)S(1)}, u32[]{:S(2)}, u32[]{:S(2)}) collective-permute-start(bf16[8,2,16,512]{3,2,1,0:T(8,128)(2,1)S(1)} %incoming_left.1.left_ref), channel_id=1, source_target_pairs={{0,1},{1,0},{2,3},{3,2},{4,5},{5,4},{6,7},{7,6},{8,9},{9,8},{10,11... | collective-permute-start | bytes 786440 | tf_op jit(solution)/shard_map/ppermute | solution.py:309

commit v3 on v2

--- a/solution.py
+++ b/solution.py
@@ -193,22 +193,23 @@
     return store
 
 
-def outgoing_product(ref, left, right, total):
-    gather_rows(ref, 0, keep_in(left))
-    gather_rows(ref, 1, keep_in(right))
+def outgoing_share_kernel(own_ref, mine_ref, theirs_ref, left, right, total):
+    gather_rows(own_ref, 0, keep_in(left))
+    gather_rows(own_ref, 1, keep_in(right))
     tokens = left.shape[-1]
     lefts, rights = left[...].reshape(-1, tokens), right[...].reshape(-1, tokens)
     total[...] = lax.dot_general(
         rights, lefts, (((0,), (0,)), ((), ())), preferred_element_type=F32
     ).reshape(total.shape)
-    return total[:, :, lax.axis_index("core")]
-
-
-def outgoing_own_kernel(
-    own_ref, pair_ref, normed_ref, gate_out, proj_in, gate_in, vectors_ref,
-    partial_ref, prior_ref, gates_ref, weights_ref, columns_ref, left, right, total,
+    core = lax.axis_index("core")
+    theirs_ref[...] = total[:, :, 1 - core].astype(BF)
+    mine_ref[...] = total[:, :, core]
+
+
+def aside_kernel(
+    pair_ref, normed_ref, gate_out, proj_in, gate_in, vectors_ref,
+    prior_ref, gates_ref, weights_ref, columns_ref,
 ):
-    partial_ref[...] = outgoing_product(own_ref, left, right, total)
     gates_of(normed_ref, gate_out, gates_ref)
     for s in range(ROWS):
         prior_ref[s] = tokens_of(pair_ref, s)
@@ -219,8 +220,8 @@
             columns_ref[layer, n] = jnp.broadcast_to(row_vec, (LANES, LANES)).T
 
 
-def outgoing_kernel(other_ref, partial_ref, out_ref, left, right, total):
-    scatter_rows(partial_ref[...] + outgoing_product(other_ref, left, right, total), out_ref)
+def outgoing_kernel(mine_ref, other_ref, out_ref):
+    scatter_rows(mine_ref[...] + other_ref[...].astype(F32), out_ref)
 
 
 def incoming_left_kernel(own_ref, left_ref):
@@ -329,26 +330,34 @@
     ))
 
     mine, pairs, normed = lax.optimization_barrier((exchange(sent), pairs, normed))
-    other = swap_cores(mine)
+    mine, theirs = call(
+        outgoing_share_kernel,
+        [whole(sent_by_chip.shape)],
+        [shape(own_columns, F32), shape(own_columns, BF)],
+        [own_half, own_half, total],
+        "outgoing_share",
+    )(mine.reshape(sent_by_chip.shape))
+    mine, theirs, pairs, normed = lax.optimization_barrier((mine, theirs, pairs, normed))
+    other = swap_cores(theirs)
     made = call(
-        outgoing_own_kernel,
+        aside_kernel,
         [
-            whole(sent_by_chip.shape), whole(pairs.shape), whole(kept.shape), layer_of(gate_out, 0),
+            whole(pairs.shape), whole(kept.shape), layer_of(gate_out, 0),
             layer_of(proj_in, 1), layer_of(gate_in, 1), whole(rows.shape),
         ],
-        [shape(own_columns, F32), kept_wide, kept_wide, joined, columns],
-        [own_half, own_half, total],
-        "outgoing_own",
+        [kept_wide, kept_wide, joined, columns],
+        [],
+        "aside",
         flops,
-    )(mine.reshape(sent_by_chip.shape), pairs, normed, gate_out, proj_in, gate_in, vectors)
-    other, (partial, prior, gates, second_weights, column_vectors) = lax.optimization_barrier((other, made))
+    )(pairs, normed, gate_out, proj_in, gate_in, vectors)
+    other, (prior, gates, second_weights, column_vectors) = lax.optimization_barrier((other, made))
     (result,) = call(
         outgoing_kernel,
-        [whole(sent_by_chip.shape), whole(own_columns)],
+        [whole(own_columns)] * 2,
         [back_by_chip],
-        [own_half, own_half, total],
+        [],
         "outgoing",
-    )(other.reshape(sent_by_chip.shape), partial)
+    )(mine, other)
     combined = exchange(result.reshape(back.shape))
     sent, normed, first_pass = call(
         second_kernel,

time: 105 us -> 105 us (level)
  no operation moved by 1% of the time
where the time goes in v3:
time: 105 us; the launch traced here: 104 us
  blocking collectives  89.8 us (86%)
  Pallas kernels  7.38 us (7%)
  starting transfers between devices  5.51 us (5%)
  waiting for transfers between devices  1.63 us (2%)
    all_to_all x4, blocking collectives, exchange(): return lax.all_to_all(x, axes, 0, 0, axis_index_groups=groups, tiled=True)  89.8 us
    ppermute x2, starting transfers between devices, swap_cores(): return lax.ppermute(x, 'core', [(0, 1), (1, 0)])  5.51 us
    pallas_call x1, Pallas kernels, on_device(): call(first_kernel, [HBM] * 9, [send, kept, rows, rows], [pltpu.VMEM(pairs...  2.2 us
  transfers between devices with their start and end apart: 2, of which 2 were waited for; matrix products, arithmetic and copies ran while one was open for 0% of the time, Pallas kernels for 1%

profile of v3, /device:TPU:1, one launch (start us, length us, event | category | flops | bytes accessed | tf_op | source)
XLA Modules:
  0.0 104.4 jit_solution(18289766284506014344)
XLA Ops:
  0.0 2.2 %project_first.1 = (bf16[128,16,128]{2,1,0:T(8,128)(2,1)S(1)}, bf16[8,128,128]{2,1,0:T(8,128)(2,1)S(1)}, f32[8,128]{1,0:T(8,128)S(1)}, f32[8,128]{1,0:T(8,128)S(1)}) custom-call(f32[1024,128]{1,0:T(8,128)} %bitcast.9, s32[512]{0:T(512)} %mask_hbm.1, s32[4,128]{1,0:T(4,128)} %bitcast.14, f32[2,128]{1,0:T(2,128)} %gain_hbm.1, f32[2,128]{1,0:T(2,128)} %shift_hbm.1, ...), custom_call_target="tpu_custom_call" | custom-call | tf_op jit(solution)/shard_map/project_first/pallas_call | solution.py:312
  2.2 0.0 copy-start.1
  2.2 0.0 copy-start.2
  2.2 0.0 copy-start.4
  2.2 28.8 %all_to_all.20 = bf16[128,16,128]{2,1,0:T(8,128)(2,1)S(1)} all-to-all(bf16[128,16,128]{2,1,0:T(8,128)(2,1)S(1)} %get-tuple-element.40), channel_id=1, replica_groups={{212,214,244,246,148,150,180,182,84,86,116,118,20,22,52,54,196,198,228,..., dimensions={0} | all-to-all | bytes 1048576 | tf_op jit(solution)/shard_map/all_to_all | solution.py:307
  31.0 0.0 copy-start
  31.0 0.8 outgoing_share.1
  31.8 2.2 %collective-permute-start = (bf16[8,2,16,512]{3,2,1,0:T(8,128)(2,1)S(1)}, bf16[8,2,16,512]{3,2,1,0:T(8,128)(2,1)S(1)}, u32[]{:S(2)}, u32[]{:S(2)}) collective-permute-start(bf16[8,2,16,512]{3,2,1,0:T(8,128)(2,1)S(1)} %get-tuple-element.48), channel_id=1, source_target_pairs={{0,1},{1,0},{2,3},{3,2},{4,5},{5,4},{6,7},{7,6},{8,9},{9,8},{10,11... | collective-permute-start | bytes 786440 | tf_op jit(solution)/shard_map/ppermute | solution.py:310
  34.0 0.0 copy-done.1
  34.0 0.0 copy-done.2
  34.0 0.0 copy-done.4
  34.0 0.0 copy-done
  34.0 0.4 aside.1
  34.4 0.7 collective-permute-done.other_ref
  35.2 0.2 outgoing.1
  35.3 0.0 copy-start.3
  35.3 19.2 %all_to_all.21.back_ref = bf16[128,8,128]{2,1,0:T(8,128)(2,1)S(1)} all-to-all(bf16[128,8,128]{2,1,0:T(8,128)(2,1)S(1)} %bitcast.13), channel_id=1, replica_groups={{212,214,244,246,148,150,180,182,84,86,116,118,20,22,52,54,196,198,228,..., dimensions={0} | all-to-all | bytes 524288 | tf_op jit(solution)/shard_map/all_to_all | solution.py:307
  54.5 0.0 copy-done.3
  54.5 1.6 %finish_and_project.1 = (bf16[128,16,128]{2,1,0:T(8,128)(2,1)S(1)}, bf16[8,128,128]{2,1,0:T(8,128)(2,1)S(1)}, f32[8,128,128]{2,1,0:T(8,128)S(1)}) custom-call(bf16[128,8,128]{2,1,0:T(8,128)(2,1)S(1)} %all_to_all.21.back_ref, f32[8,128,128]{2,1,0:T(8,128)S(1)} %get-tuple-element.57.prior_ref, f32[8,128,128]{2,1,0:T(8,128)S(1)} %get-tuple-element.58.gates_ref, ...), custom_call_target="tpu_custom_call" | custom-call | tf_op jit(solution)/shard_map/finish_and_project/pallas_call | solution.py:362
  56.2 22.7 %all_to_all.22 = bf16[128,16,128]{2,1,0:T(8,128)(2,1)S(1)} all-to-all(bf16[128,16,128]{2,1,0:T(8,128)(2,1)S(1)} %get-tuple-element.62), channel_id=1, replica_groups={{212,214,244,246,148,150,180,182,84,86,116,118,20,22,52,54,196,198,228,..., dimensions={0} | all-to-all | bytes 1048576 | tf_op jit(solution)/shard_map/all_to_all | solution.py:307
  78.9 0.1 incoming_left.1.left_ref
  79.0 3.3 %collective-permute-start.1 = (bf16[8,2,16,512]{3,2,1,0:T(8,128)(2,1)S(1)}, bf16[8,2,16,512]{3,2,1,0:T(8,128)(2,1)S(1)}, u32[]{:S(2)}, u32[]{:S(2)}) collective-permute-start(bf16[8,2,16,512]{3,2,1,0:T(8,128)(2,1)S(1)} %incoming_left.1.left_ref), channel_id=1, source_target_pairs={{0,1},{1,0},{2,3},{3,2},{4,5},{5,4},{6,7},{7,6},{8,9},{9,8},{10,11... | collective-permute-start | bytes 786440 | tf_op jit(solution)/shard_map/ppermute | solution.py:310
  82.4 0.3 incoming_right.1
  82.7 0.9 collective-permute-done.1.other_ref
  83.5 0.4 incoming.1
  84.0 19.1 %all_to_all.23.back_ref = bf16[128,8,128]{2,1,0:T(8,128)(2,1)S(1)} all-to-all(bf16[128,8,128]{2,1,0:T(8,128)(2,1)S(1)} %bitcast.12), channel_id=1, replica_groups={{212,214,244,246,148,150,180,182,84,86,116,118,20,22,52,54,196,198,228,..., dimensions={0} | all-to-all | bytes 524288 | tf_op jit(solution)/shard_map/all_to_all | solution.py:307
  103.1 1.3 %finish.1 = f32[1024,128]{1,0:T(8,128)} custom-call(bf16[128,8,128]{2,1,0:T(8,128)(2,1)S(1)} %all_to_all.23.back_ref, f32[8,128,128]{2,1,0:T(8,128)S(1)} %get-tuple-element.73.pass_ref, f32[8,128,128]{2,1,0:T(8,128)S(1)} %get-tuple-element.74.gates_ref, f32[2,2,128,128]{3,2,1,0:T(8,128)S(1)} %get-tuple-element.60.columns_ref, bf16[2,128,128]{2,1,0:T(8,128)(2,1)S(1)} %copy-done.3), custom_call_target="tpu_custom_call" | custom-call | tf_op jit(solution)/shard_map/finish/pallas_call | solution.py:400
Async XLA Ops:
  2.2 31.8 %copy-start.1 = (bf16[2,128,256]{2,1,0:T(8,128)(2,1)S(1)}, bf16[2,128,256]{2,1,0:T(8,128)(2,1)}, u32[]{:S(2)}) copy-start(bf16[2,128,256]{2,1,0:T(8,128)(2,1)} %proj_in.1) | copy-start | bytes 393220
  2.2 31.8 %copy-start.2 = (bf16[2,128,256]{2,1,0:T(8,128)(2,1)S(1)}, bf16[2,128,256]{2,1,0:T(8,128)(2,1)}, u32[]{:S(2)}) copy-start(bf16[2,128,256]{2,1,0:T(8,128)(2,1)} %gate_in.1) | copy-start | bytes 393220
  2.2 31.8 %copy-start.4 = (bf16[2,128,128]{2,1,0:T(8,128)(2,1)S(1)}, bf16[2,128,128]{2,1,0:T(8,128)(2,1)}, u32[]{:S(2)}) copy-start(bf16[2,128,128]{2,1,0:T(8,128)(2,1)} %gate_out.3) | copy-start | bytes 196612
  31.0 3.0 %copy-start = (f32[64,16,128]{2,1,0:T(8,128)S(1)}, f32[64,16,128]{2,1,0:T(8,128)}, u32[]{:S(2)}) copy-start(f32[64,16,128]{2,1,0:T(8,128)} %param.10) | copy-start | bytes 1572868
  31.8 3.3 %collective-permute-start = (bf16[8,2,16,512]{3,2,1,0:T(8,128)(2,1)S(1)}, bf16[8,2,16,512]{3,2,1,0:T(8,128)(2,1)S(1)}, u32[]{:S(2)}, u32[]{:S(2)}) collective-permute-start(bf16[8,2,16,512]{3,2,1,0:T(8,128)(2,1)S(1)} %get-tuple-element.48), channel_id=1, source_target_pairs={{0,1},{1,0},{2,3},{3,2},{4,5},{5,4},{6,7},{7,6},{8,9},{9,8},{10,11... | collective-permute-start | bytes 786440 | tf_op jit(solution)/shard_map/ppermute | solution.py:310
  35.3 19.2 %copy-start.3 = (bf16[2,128,128]{2,1,0:T(8,128)(2,1)S(1)}, bf16[2,128,128]{2,1,0:T(8,128)(2,1)}, u32[]{:S(2)}) copy-start(bf16[2,128,128]{2,1,0:T(8,128)(2,1)} %proj_out.3) | copy-start | bytes 196612
  79.0 4.5 %collective-permute-start.1 = (bf16[8,2,16,512]{3,2,1,0:T(8,128)(2,1)S(1)}, bf16[8,2,16,512]{3,2,1,0:T(8,128)(2,1)S(1)}, u32[]{:S(2)}, u32[]{:S(2)}) collective-permute-start(bf16[8,2,16,512]{3,2,1,0:T(8,128)(2,1)S(1)} %incoming_left.1.left_ref), channel_id=1, source_target_pairs={{0,1},{1,0},{2,3},{3,2},{4,5},{5,4},{6,7},{7,6},{8,9},{9,8},{10,11... | collective-permute-start | bytes 786440 | tf_op jit(solution)/shard_map/ppermute | solution.py:310

commit v4 on v3

--- a/solution.py
+++ b/solution.py
@@ -44,7 +44,7 @@
     normed = layer_norm(chunk, gain, shift, -1).astype(BF)
     normed_ref[s : s + 2] = normed.reshape(2, LANES, LANES)
     both = lax.dot_general(weights, normed, (((1,), (1,)), ((), ())), preferred_element_type=F32)
-    halves = sigmoid(both[2 * LANES :]) * both[: 2 * LANES] * weight
+    halves = (jnp.tanh(both[2 * LANES :]) + 1.0) * (both[: 2 * LANES] * weight)
     for n in range(2):
         part = halves[:, n * LANES : (n + 1) * LANES]
         staged[pl.ds(s + n, LANES, stride=2 * ROWS), :] = part[:LANES]
@@ -52,7 +52,7 @@
 
 
 def joined_weights(proj_in, gate_in):
-    return jnp.concatenate([proj_in.T, gate_in.T], axis=0)
+    return jnp.concatenate([proj_in.T, gate_in.T * jnp.bfloat16(0.5)], axis=0)
 
 
 def pair_of(ref, s):
@@ -110,7 +110,7 @@
         for n in range(2):
             first = mask_smem[begin + s + n].astype(F32)
             second = mask_smem[begin + ROWS + s + n].astype(F32)
-            weight = own * jnp.where(low, first, second)
+            weight = own * jnp.where(low, 0.5 * first, 0.5 * second)
             weight_ref[pl.ds(s + n, 1), :] = weight
             both.append(weight)
         chunk = jnp.concatenate([tokens_of(pair_ref, s), tokens_of(pair_ref, s + 1)], axis=0)

time: 105 us -> 105 us (level)
  no operation moved by 1% of the time
where the time goes in v4:
time: 105 us; the launch traced here: 104 us
  blocking collectives  89.8 us (86%)
  Pallas kernels  7.27 us (7%)
  starting transfers between devices  5.51 us (5%)
  waiting for transfers between devices  1.63 us (2%)
    all_to_all x4, blocking collectives, exchange(): return lax.all_to_all(x, axes, 0, 0, axis_index_groups=groups, tiled=True)  89.8 us
    ppermute x2, starting transfers between devices, swap_cores(): return lax.ppermute(x, 'core', [(0, 1), (1, 0)])  5.51 us
    pallas_call x1, Pallas kernels, on_device(): call(first_kernel, [HBM] * 9, [send, kept, rows, rows], [pltpu.VMEM(pairs...  2.14 us
  transfers between devices with their start and end apart: 2, of which 2 were waited for; matrix products, arithmetic and copies ran while one was open for 0% of the time, Pallas kernels for 1%

profile of v4, /device:TPU:1, one launch (start us, length us, event | category | flops | bytes accessed | tf_op | source)
XLA Modules:
  0.0 104.3 jit_solution(14824449182837184037)
XLA Ops:
  0.0 2.1 %project_first.1 = (bf16[128,16,128]{2,1,0:T(8,128)(2,1)S(1)}, bf16[8,128,128]{2,1,0:T(8,128)(2,1)S(1)}, f32[8,128]{1,0:T(8,128)S(1)}, f32[8,128]{1,0:T(8,128)S(1)}) custom-call(f32[1024,128]{1,0:T(8,128)} %bitcast.9, s32[512]{0:T(512)} %mask_hbm.1, s32[4,128]{1,0:T(4,128)} %bitcast.14, f32[2,128]{1,0:T(2,128)} %gain_hbm.1, f32[2,128]{1,0:T(2,128)} %shift_hbm.1, ...), custom_call_target="tpu_custom_call" | custom-call | tf_op jit(solution)/shard_map/project_first/pallas_call | solution.py:312
  2.2 0.0 copy-start.1
  2.2 0.0 copy-start.2
  2.2 0.0 copy-start.4
  2.2 28.8 %all_to_all.20 = bf16[128,16,128]{2,1,0:T(8,128)(2,1)S(1)} all-to-all(bf16[128,16,128]{2,1,0:T(8,128)(2,1)S(1)} %get-tuple-element.40), channel_id=1, replica_groups={{212,214,244,246,148,150,180,182,84,86,116,118,20,22,52,54,196,198,228,..., dimensions={0} | all-to-all | bytes 1048576 | tf_op jit(solution)/shard_map/all_to_all | solution.py:307
  31.0 0.0 copy-start
  31.0 0.8 outgoing_share.1
  31.8 2.2 %collective-permute-start = (bf16[8,2,16,512]{3,2,1,0:T(8,128)(2,1)S(1)}, bf16[8,2,16,512]{3,2,1,0:T(8,128)(2,1)S(1)}, u32[]{:S(2)}, u32[]{:S(2)}) collective-permute-start(bf16[8,2,16,512]{3,2,1,0:T(8,128)(2,1)S(1)} %get-tuple-element.48), channel_id=1, source_target_pairs={{0,1},{1,0},{2,3},{3,2},{4,5},{5,4},{6,7},{7,6},{8,9},{9,8},{10,11... | collective-permute-start | bytes 786440 | tf_op jit(solution)/shard_map/ppermute | solution.py:310
  33.9 0.0 copy-done.1
  33.9 0.0 copy-done.2
  34.0 0.0 copy-done.4
  34.0 0.0 copy-done
  34.0 0.4 aside.1
  34.4 0.7 collective-permute-done.other_ref
  35.1 0.2 outgoing.1
  35.3 0.0 copy-start.3
  35.3 19.2 %all_to_all.21.back_ref = bf16[128,8,128]{2,1,0:T(8,128)(2,1)S(1)} all-to-all(bf16[128,8,128]{2,1,0:T(8,128)(2,1)S(1)} %bitcast.13), channel_id=1, replica_groups={{212,214,244,246,148,150,180,182,84,86,116,118,20,22,52,54,196,198,228,..., dimensions={0} | all-to-all | bytes 524288 | tf_op jit(solution)/shard_map/all_to_all | solution.py:307
  54.5 0.0 copy-done.3
  54.5 1.6 %finish_and_project.1 = (bf16[128,16,128]{2,1,0:T(8,128)(2,1)S(1)}, bf16[8,128,128]{2,1,0:T(8,128)(2,1)S(1)}, f32[8,128,128]{2,1,0:T(8,128)S(1)}) custom-call(bf16[128,8,128]{2,1,0:T(8,128)(2,1)S(1)} %all_to_all.21.back_ref, f32[8,128,128]{2,1,0:T(8,128)S(1)} %get-tuple-element.57.prior_ref, f32[8,128,128]{2,1,0:T(8,128)S(1)} %get-tuple-element.58.gates_ref, ...), custom_call_target="tpu_custom_call" | custom-call | tf_op jit(solution)/shard_map/finish_and_project/pallas_call | solution.py:362
  56.1 22.7 %all_to_all.22 = bf16[128,16,128]{2,1,0:T(8,128)(2,1)S(1)} all-to-all(bf16[128,16,128]{2,1,0:T(8,128)(2,1)S(1)} %get-tuple-element.62), channel_id=1, replica_groups={{212,214,244,246,148,150,180,182,84,86,116,118,20,22,52,54,196,198,228,..., dimensions={0} | all-to-all | bytes 1048576 | tf_op jit(solution)/shard_map/all_to_all | solution.py:307
  78.8 0.1 incoming_left.1.left_ref
  78.9 3.3 %collective-permute-start.1 = (bf16[8,2,16,512]{3,2,1,0:T(8,128)(2,1)S(1)}, bf16[8,2,16,512]{3,2,1,0:T(8,128)(2,1)S(1)}, u32[]{:S(2)}, u32[]{:S(2)}) collective-permute-start(bf16[8,2,16,512]{3,2,1,0:T(8,128)(2,1)S(1)} %incoming_left.1.left_ref), channel_id=1, source_target_pairs={{0,1},{1,0},{2,3},{3,2},{4,5},{5,4},{6,7},{7,6},{8,9},{9,8},{10,11... | collective-permute-start | bytes 786440 | tf_op jit(solution)/shard_map/ppermute | solution.py:310
  82.3 0.3 incoming_right.1
  82.5 0.9 collective-permute-done.1.other_ref
  83.4 0.4 incoming.1
  83.9 19.1 %all_to_all.23.back_ref = bf16[128,8,128]{2,1,0:T(8,128)(2,1)S(1)} all-to-all(bf16[128,8,128]{2,1,0:T(8,128)(2,1)S(1)} %bitcast.12), channel_id=1, replica_groups={{212,214,244,246,148,150,180,182,84,86,116,118,20,22,52,54,196,198,228,..., dimensions={0} | all-to-all | bytes 524288 | tf_op jit(solution)/shard_map/all_to_all | solution.py:307
  102.9 1.3 %finish.1 = f32[1024,128]{1,0:T(8,128)} custom-call(bf16[128,8,128]{2,1,0:T(8,128)(2,1)S(1)} %all_to_all.23.back_ref, f32[8,128,128]{2,1,0:T(8,128)S(1)} %get-tuple-element.73.pass_ref, f32[8,128,128]{2,1,0:T(8,128)S(1)} %get-tuple-element.74.gates_ref, f32[2,2,128,128]{3,2,1,0:T(8,128)S(1)} %get-tuple-element.60.columns_ref, bf16[2,128,128]{2,1,0:T(8,128)(2,1)S(1)} %copy-done.3), custom_call_target="tpu_custom_call" | custom-call | tf_op jit(solution)/shard_map/finish/pallas_call | solution.py:400
Async XLA Ops:
  2.2 31.8 %copy-start.1 = (bf16[2,128,256]{2,1,0:T(8,128)(2,1)S(1)}, bf16[2,128,256]{2,1,0:T(8,128)(2,1)}, u32[]{:S(2)}) copy-start(bf16[2,128,256]{2,1,0:T(8,128)(2,1)} %proj_in.1) | copy-start | bytes 393220
  2.2 31.8 %copy-start.2 = (bf16[2,128,256]{2,1,0:T(8,128)(2,1)S(1)}, bf16[2,128,256]{2,1,0:T(8,128)(2,1)}, u32[]{:S(2)}) copy-start(bf16[2,128,256]{2,1,0:T(8,128)(2,1)} %gate_in.1) | copy-start | bytes 393220
  2.2 31.8 %copy-start.4 = (bf16[2,128,128]{2,1,0:T(8,128)(2,1)S(1)}, bf16[2,128,128]{2,1,0:T(8,128)(2,1)}, u32[]{:S(2)}) copy-start(bf16[2,128,128]{2,1,0:T(8,128)(2,1)} %gate_out.3) | copy-start | bytes 196612
  31.0 3.0 %copy-start = (f32[64,16,128]{2,1,0:T(8,128)S(1)}, f32[64,16,128]{2,1,0:T(8,128)}, u32[]{:S(2)}) copy-start(f32[64,16,128]{2,1,0:T(8,128)} %param.10) | copy-start | bytes 1572868
  31.8 3.3 %collective-permute-start = (bf16[8,2,16,512]{3,2,1,0:T(8,128)(2,1)S(1)}, bf16[8,2,16,512]{3,2,1,0:T(8,128)(2,1)S(1)}, u32[]{:S(2)}, u32[]{:S(2)}) collective-permute-start(bf16[8,2,16,512]{3,2,1,0:T(8,128)(2,1)S(1)} %get-tuple-element.48), channel_id=1, source_target_pairs={{0,1},{1,0},{2,3},{3,2},{4,5},{5,4},{6,7},{7,6},{8,9},{9,8},{10,11... | collective-permute-start | bytes 786440 | tf_op jit(solution)/shard_map/ppermute | solution.py:310
  35.3 19.2 %copy-start.3 = (bf16[2,128,128]{2,1,0:T(8,128)(2,1)S(1)}, bf16[2,128,128]{2,1,0:T(8,128)(2,1)}, u32[]{:S(2)}) copy-start(bf16[2,128,128]{2,1,0:T(8,128)(2,1)} %proj_out.3) | copy-start | bytes 196612
  78.9 4.5 %collective-permute-start.1 = (bf16[8,2,16,512]{3,2,1,0:T(8,128)(2,1)S(1)}, bf16[8,2,16,512]{3,2,1,0:T(8,128)(2,1)S(1)}, u32[]{:S(2)}, u32[]{:S(2)}) collective-permute-start(bf16[8,2,16,512]{3,2,1,0:T(8,128)(2,1)S(1)} %incoming_left.1.left_ref), channel_id=1, source_target_pairs={{0,1},{1,0},{2,3},{3,2},{4,5},{5,4},{6,7},{7,6},{8,9},{9,8},{10,11... | collective-permute-start | bytes 786440 | tf_op jit(solution)/shard_map/ppermute | solution.py:310

commit v5 on v4

--- a/solution.py
+++ b/solution.py
@@ -14,7 +14,7 @@
 BF, F32 = jnp.bfloat16, jnp.float32
 VMEM_LIMIT = 40 * 1024 * 1024
 ORDER = ("z", "h", "x", "y")
-LISTS = {"z": (5, 1, 6, 2, 7, 3, 0, 4), "y": (0, 1), "h": (1, 0), "x": (2, 3, 0, 1)}
+LISTS = {"z": (5, 1, 4, 0, 3, 7, 2, 6), "y": (0, 1), "h": (1, 0), "x": (2, 3, 0, 1)}
 
 
 def sigmoid(x):

time: 105 us -> 105 us (level)
  blocking collectives: 89.8 us -> 91.3 us
    all_to_all x4, blocking collectives: 89.8 us -> 91.3 us  [exchange(): return lax.all_to_all(x, axes, 0, 0, axis_index_groups=groups, tiled=True)]
where the time goes in v5:
time: 105 us
  blocking collectives  91.3 us (87%)
  Pallas kernels  7.27 us (7%)
  starting transfers between devices  4.73 us (5%)
  waiting for transfers between devices  1.63 us (2%)
    all_to_all x4, blocking collectives, exchange(): return lax.all_to_all(x, axes, 0, 0, axis_index_groups=groups, tiled=True)  91.3 us
    ppermute x2, starting transfers between devices, swap_cores(): return lax.ppermute(x, 'core', [(0, 1), (1, 0)])  4.73 us
    pallas_call x1, Pallas kernels, on_device(): call(first_kernel, [HBM] * 9, [send, kept, rows, rows], [pltpu.VMEM(pairs...  2.14 us
  transfers between devices with their start and end apart: 2, of which 2 were waited for; matrix products, arithmetic and copies ran while one was open for 0% of the time, Pallas kernels for 1%

profile of v5, /device:TPU:1, one launch (start us, length us, event | category | flops | bytes accessed | tf_op | source)
XLA Modules:
  0.0 105.0 jit_solution(13471428391387473260)
XLA Ops:
  0.0 2.1 %project_first.1 = (bf16[128,16,128]{2,1,0:T(8,128)(2,1)S(1)}, bf16[8,128,128]{2,1,0:T(8,128)(2,1)S(1)}, f32[8,128]{1,0:T(8,128)S(1)}, f32[8,128]{1,0:T(8,128)S(1)}) custom-call(f32[1024,128]{1,0:T(8,128)} %bitcast.9, s32[512]{0:T(512)} %mask_hbm.1, s32[4,128]{1,0:T(4,128)} %bitcast.14, f32[2,128]{1,0:T(2,128)} %gain_hbm.1, f32[2,128]{1,0:T(2,128)} %shift_hbm.1, ...), custom_call_target="tpu_custom_call" | custom-call | tf_op jit(solution)/shard_map/project_first/pallas_call | solution.py:312
  2.2 0.0 copy-start.1
  2.2 0.0 copy-start.2
  2.2 0.0 copy-start.4
  2.2 29.1 %all_to_all.20 = bf16[128,16,128]{2,1,0:T(8,128)(2,1)S(1)} all-to-all(bf16[128,16,128]{2,1,0:T(8,128)(2,1)S(1)} %get-tuple-element.40), channel_id=1, replica_groups={{212,214,244,246,148,150,180,182,84,86,116,118,20,22,52,54,196,198,228,..., dimensions={0} | all-to-all | bytes 1048576 | tf_op jit(solution)/shard_map/all_to_all | solution.py:307
  31.3 0.0 copy-start
  31.3 0.8 outgoing_share.1
  32.0 2.1 %collective-permute-start = (bf16[8,2,16,512]{3,2,1,0:T(8,128)(2,1)S(1)}, bf16[8,2,16,512]{3,2,1,0:T(8,128)(2,1)S(1)}, u32[]{:S(2)}, u32[]{:S(2)}) collective-permute-start(bf16[8,2,16,512]{3,2,1,0:T(8,128)(2,1)S(1)} %get-tuple-element.48), channel_id=1, source_target_pairs={{0,1},{1,0},{2,3},{3,2},{4,5},{5,4},{6,7},{7,6},{8,9},{9,8},{10,11... | collective-permute-start | bytes 786440 | tf_op jit(solution)/shard_map/ppermute | solution.py:310
  34.2 0.0 copy-done.1
  34.2 0.0 copy-done.2
  34.2 0.0 copy-done.4
  34.2 0.0 copy-done
  34.2 0.4 aside.1
  34.6 0.7 collective-permute-done.other_ref
  35.3 0.2 outgoing.1
  35.5 0.0 copy-start.3
  35.5 19.2 %all_to_all.21.back_ref = bf16[128,8,128]{2,1,0:T(8,128)(2,1)S(1)} all-to-all(bf16[128,8,128]{2,1,0:T(8,128)(2,1)S(1)} %bitcast.13), channel_id=1, replica_groups={{212,214,244,246,148,150,180,182,84,86,116,118,20,22,52,54,196,198,228,..., dimensions={0} | all-to-all | bytes 524288 | tf_op jit(solution)/shard_map/all_to_all | solution.py:307
  54.7 0.0 copy-done.3
  54.7 1.6 %finish_and_project.1 = (bf16[128,16,128]{2,1,0:T(8,128)(2,1)S(1)}, bf16[8,128,128]{2,1,0:T(8,128)(2,1)S(1)}, f32[8,128,128]{2,1,0:T(8,128)S(1)}) custom-call(bf16[128,8,128]{2,1,0:T(8,128)(2,1)S(1)} %all_to_all.21.back_ref, f32[8,128,128]{2,1,0:T(8,128)S(1)} %get-tuple-element.57.prior_ref, f32[8,128,128]{2,1,0:T(8,128)S(1)} %get-tuple-element.58.gates_ref, ...), custom_call_target="tpu_custom_call" | custom-call | tf_op jit(solution)/shard_map/finish_and_project/pallas_call | solution.py:362
  56.3 24.0 %all_to_all.22 = bf16[128,16,128]{2,1,0:T(8,128)(2,1)S(1)} all-to-all(bf16[128,16,128]{2,1,0:T(8,128)(2,1)S(1)} %get-tuple-element.62), channel_id=1, replica_groups={{212,214,244,246,148,150,180,182,84,86,116,118,20,22,52,54,196,198,228,..., dimensions={0} | all-to-all | bytes 1048576 | tf_op jit(solution)/shard_map/all_to_all | solution.py:307
  80.3 0.1 incoming_left.1.left_ref
  80.4 2.6 %collective-permute-start.1 = (bf16[8,2,16,512]{3,2,1,0:T(8,128)(2,1)S(1)}, bf16[8,2,16,512]{3,2,1,0:T(8,128)(2,1)S(1)}, u32[]{:S(2)}, u32[]{:S(2)}) collective-permute-start(bf16[8,2,16,512]{3,2,1,0:T(8,128)(2,1)S(1)} %incoming_left.1.left_ref), channel_id=1, source_target_pairs={{0,1},{1,0},{2,3},{3,2},{4,5},{5,4},{6,7},{7,6},{8,9},{9,8},{10,11... | collective-permute-start | bytes 786440 | tf_op jit(solution)/shard_map/ppermute | solution.py:310
  83.0 0.3 incoming_right.1
  83.3 0.9 collective-permute-done.1.other_ref
  84.2 0.4 incoming.1
  84.7 19.0 %all_to_all.23.back_ref = bf16[128,8,128]{2,1,0:T(8,128)(2,1)S(1)} all-to-all(bf16[128,8,128]{2,1,0:T(8,128)(2,1)S(1)} %bitcast.12), channel_id=1, replica_groups={{212,214,244,246,148,150,180,182,84,86,116,118,20,22,52,54,196,198,228,..., dimensions={0} | all-to-all | bytes 524288 | tf_op jit(solution)/shard_map/all_to_all | solution.py:307
  103.7 1.3 %finish.1 = f32[1024,128]{1,0:T(8,128)} custom-call(bf16[128,8,128]{2,1,0:T(8,128)(2,1)S(1)} %all_to_all.23.back_ref, f32[8,128,128]{2,1,0:T(8,128)S(1)} %get-tuple-element.73.pass_ref, f32[8,128,128]{2,1,0:T(8,128)S(1)} %get-tuple-element.74.gates_ref, f32[2,2,128,128]{3,2,1,0:T(8,128)S(1)} %get-tuple-element.60.columns_ref, bf16[2,128,128]{2,1,0:T(8,128)(2,1)S(1)} %copy-done.3), custom_call_target="tpu_custom_call" | custom-call | tf_op jit(solution)/shard_map/finish/pallas_call | solution.py:400
Async XLA Ops:
  2.2 32.0 %copy-start.1 = (bf16[2,128,256]{2,1,0:T(8,128)(2,1)S(1)}, bf16[2,128,256]{2,1,0:T(8,128)(2,1)}, u32[]{:S(2)}) copy-start(bf16[2,128,256]{2,1,0:T(8,128)(2,1)} %proj_in.1) | copy-start | bytes 393220
  2.2 32.0 %copy-start.2 = (bf16[2,128,256]{2,1,0:T(8,128)(2,1)S(1)}, bf16[2,128,256]{2,1,0:T(8,128)(2,1)}, u32[]{:S(2)}) copy-start(bf16[2,128,256]{2,1,0:T(8,128)(2,1)} %gate_in.1) | copy-start | bytes 393220
  2.2 32.0 %copy-start.4 = (bf16[2,128,128]{2,1,0:T(8,128)(2,1)S(1)}, bf16[2,128,128]{2,1,0:T(8,128)(2,1)}, u32[]{:S(2)}) copy-start(bf16[2,128,128]{2,1,0:T(8,128)(2,1)} %gate_out.3) | copy-start | bytes 196612
  31.3 2.9 %copy-start = (f32[64,16,128]{2,1,0:T(8,128)S(1)}, f32[64,16,128]{2,1,0:T(8,128)}, u32[]{:S(2)}) copy-start(f32[64,16,128]{2,1,0:T(8,128)} %param.10) | copy-start | bytes 1572868
  32.0 3.3 %collective-permute-start = (bf16[8,2,16,512]{3,2,1,0:T(8,128)(2,1)S(1)}, bf16[8,2,16,512]{3,2,1,0:T(8,128)(2,1)S(1)}, u32[]{:S(2)}, u32[]{:S(2)}) collective-permute-start(bf16[8,2,16,512]{3,2,1,0:T(8,128)(2,1)S(1)} %get-tuple-element.48), channel_id=1, source_target_pairs={{0,1},{1,0},{2,3},{3,2},{4,5},{5,4},{6,7},{7,6},{8,9},{9,8},{10,11... | collective-permute-start | bytes 786440 | tf_op jit(solution)/shard_map/ppermute | solution.py:310
  35.5 19.2 %copy-start.3 = (bf16[2,128,128]{2,1,0:T(8,128)(2,1)S(1)}, bf16[2,128,128]{2,1,0:T(8,128)(2,1)}, u32[]{:S(2)}) copy-start(bf16[2,128,128]{2,1,0:T(8,128)(2,1)} %proj_out.3) | copy-start | bytes 196612
  80.4 3.8 %collective-permute-start.1 = (bf16[8,2,16,512]{3,2,1,0:T(8,128)(2,1)S(1)}, bf16[8,2,16,512]{3,2,1,0:T(8,128)(2,1)S(1)}, u32[]{:S(2)}, u32[]{:S(2)}) collective-permute-start(bf16[8,2,16,512]{3,2,1,0:T(8,128)(2,1)S(1)} %incoming_left.1.left_ref), channel_id=1, source_target_pairs={{0,1},{1,0},{2,3},{3,2},{4,5},{5,4},{6,7},{7,6},{8,9},{9,8},{10,11... | collective-permute-start | bytes 786440 | tf_op jit(solution)/shard_map/ppermute | solution.py:310

commit v6 on v4

--- a/solution.py
+++ b/solution.py
@@ -97,7 +97,7 @@
     for copy in copies[:2]:
         copy.wait()
     weights = joined_weights(proj_in[...], gate_in[...])
-    for copy in copies[2:]:
+    for copy in copies[2:7]:
         copy.wait()
     row, core = lax.axis_index(("h", "x")), lax.axis_index("core")
     chip = lax.axis_index("z") * 2 + lax.axis_index("y")
@@ -117,6 +117,8 @@
         weight = jnp.concatenate(both, axis=1)
         project(chunk, s, weight, gain[0:1], shift[0:1], weights, staged, normed_ref)
     send_ref[...] = staged[...].astype(BF).reshape(send_ref.shape)
+    for copy in copies[7:]:
+        copy.wait()
     for n, ref in enumerate((gain, shift, out_gain, out_shift)):
         vectors_ref[pl.ds(2 * n, 2), :] = ref[...]
 

time: 105 us -> 105 us (level)
  no operation moved by 1% of the time
where the time goes in v6:
time: 105 us; the launch traced here: 104 us
  blocking collectives  89.8 us (86%)
  Pallas kernels  7.26 us (7%)
  starting transfers between devices  5.51 us (5%)
  waiting for transfers between devices  1.63 us (2%)
    all_to_all x4, blocking collectives, exchange(): return lax.all_to_all(x, axes, 0, 0, axis_index_groups=groups, tiled=True)  89.8 us
    ppermute x2, starting transfers between devices, swap_cores(): return lax.ppermute(x, 'core', [(0, 1), (1, 0)])  5.51 us
    pallas_call x1, Pallas kernels, on_device(): call(first_kernel, [HBM] * 9, [send, kept, rows, rows], [pltpu.VMEM(pairs...  2.14 us
  transfers between devices with their start and end apart: 2, of which 2 were waited for; matrix products, arithmetic and copies ran while one was open for 0% of the time, Pallas kernels for 1%

profile of v6, /device:TPU:1, one launch (start us, length us, event | category | flops | bytes accessed | tf_op | source)
XLA Modules:
  0.0 104.3 jit_solution(2476632022574568472)
XLA Ops:
  0.0 2.1 %project_first.1 = (bf16[128,16,128]{2,1,0:T(8,128)(2,1)S(1)}, bf16[8,128,128]{2,1,0:T(8,128)(2,1)S(1)}, f32[8,128]{1,0:T(8,128)S(1)}, f32[8,128]{1,0:T(8,128)S(1)}) custom-call(f32[1024,128]{1,0:T(8,128)} %bitcast.9, s32[512]{0:T(512)} %mask_hbm.1, s32[4,128]{1,0:T(4,128)} %bitcast.14, f32[2,128]{1,0:T(2,128)} %gain_hbm.1, f32[2,128]{1,0:T(2,128)} %shift_hbm.1, ...), custom_call_target="tpu_custom_call" | custom-call | tf_op jit(solution)/shard_map/project_first/pallas_call | solution.py:314
  2.1 0.0 copy-start.1
  2.2 0.0 copy-start.2
  2.2 0.0 copy-start.4
  2.2 28.8 %all_to_all.20 = bf16[128,16,128]{2,1,0:T(8,128)(2,1)S(1)} all-to-all(bf16[128,16,128]{2,1,0:T(8,128)(2,1)S(1)} %get-tuple-element.40), channel_id=1, replica_groups={{212,214,244,246,148,150,180,182,84,86,116,118,20,22,52,54,196,198,228,..., dimensions={0} | all-to-all | bytes 1048576 | tf_op jit(solution)/shard_map/all_to_all | solution.py:309
  31.0 0.0 copy-start
  31.0 0.8 outgoing_share.1
  31.8 2.2 %collective-permute-start = (bf16[8,2,16,512]{3,2,1,0:T(8,128)(2,1)S(1)}, bf16[8,2,16,512]{3,2,1,0:T(8,128)(2,1)S(1)}, u32[]{:S(2)}, u32[]{:S(2)}) collective-permute-start(bf16[8,2,16,512]{3,2,1,0:T(8,128)(2,1)S(1)} %get-tuple-element.48), channel_id=1, source_target_pairs={{0,1},{1,0},{2,3},{3,2},{4,5},{5,4},{6,7},{7,6},{8,9},{9,8},{10,11... | collective-permute-start | bytes 786440 | tf_op jit(solution)/shard_map/ppermute | solution.py:312
  33.9 0.0 copy-done.1
  33.9 0.0 copy-done.2
  34.0 0.0 copy-done.4
  34.0 0.0 copy-done
  34.0 0.4 aside.1
  34.4 0.7 collective-permute-done.other_ref
  35.1 0.2 outgoing.1
  35.3 0.0 copy-start.3
  35.3 19.2 %all_to_all.21.back_ref = bf16[128,8,128]{2,1,0:T(8,128)(2,1)S(1)} all-to-all(bf16[128,8,128]{2,1,0:T(8,128)(2,1)S(1)} %bitcast.13), channel_id=1, replica_groups={{212,214,244,246,148,150,180,182,84,86,116,118,20,22,52,54,196,198,228,..., dimensions={0} | all-to-all | bytes 524288 | tf_op jit(solution)/shard_map/all_to_all | solution.py:309
  54.5 0.0 copy-done.3
  54.5 1.6 %finish_and_project.1 = (bf16[128,16,128]{2,1,0:T(8,128)(2,1)S(1)}, bf16[8,128,128]{2,1,0:T(8,128)(2,1)S(1)}, f32[8,128,128]{2,1,0:T(8,128)S(1)}) custom-call(bf16[128,8,128]{2,1,0:T(8,128)(2,1)S(1)} %all_to_all.21.back_ref, f32[8,128,128]{2,1,0:T(8,128)S(1)} %get-tuple-element.57.prior_ref, f32[8,128,128]{2,1,0:T(8,128)S(1)} %get-tuple-element.58.gates_ref, ...), custom_call_target="tpu_custom_call" | custom-call | tf_op jit(solution)/shard_map/finish_and_project/pallas_call | solution.py:364
  56.1 22.7 %all_to_all.22 = bf16[128,16,128]{2,1,0:T(8,128)(2,1)S(1)} all-to-all(bf16[128,16,128]{2,1,0:T(8,128)(2,1)S(1)} %get-tuple-element.62), channel_id=1, replica_groups={{212,214,244,246,148,150,180,182,84,86,116,118,20,22,52,54,196,198,228,..., dimensions={0} | all-to-all | bytes 1048576 | tf_op jit(solution)/shard_map/all_to_all | solution.py:309
  78.8 0.1 incoming_left.1.left_ref
  78.9 3.3 %collective-permute-start.1 = (bf16[8,2,16,512]{3,2,1,0:T(8,128)(2,1)S(1)}, bf16[8,2,16,512]{3,2,1,0:T(8,128)(2,1)S(1)}, u32[]{:S(2)}, u32[]{:S(2)}) collective-permute-start(bf16[8,2,16,512]{3,2,1,0:T(8,128)(2,1)S(1)} %incoming_left.1.left_ref), channel_id=1, source_target_pairs={{0,1},{1,0},{2,3},{3,2},{4,5},{5,4},{6,7},{7,6},{8,9},{9,8},{10,11... | collective-permute-start | bytes 786440 | tf_op jit(solution)/shard_map/ppermute | solution.py:312
  82.3 0.3 incoming_right.1
  82.5 0.9 collective-permute-done.1.other_ref
  83.4 0.4 incoming.1
  83.9 19.1 %all_to_all.23.back_ref = bf16[128,8,128]{2,1,0:T(8,128)(2,1)S(1)} all-to-all(bf16[128,8,128]{2,1,0:T(8,128)(2,1)S(1)} %bitcast.12), channel_id=1, replica_groups={{212,214,244,246,148,150,180,182,84,86,116,118,20,22,52,54,196,198,228,..., dimensions={0} | all-to-all | bytes 524288 | tf_op jit(solution)/shard_map/all_to_all | solution.py:309
  102.9 1.3 %finish.1 = f32[1024,128]{1,0:T(8,128)} custom-call(bf16[128,8,128]{2,1,0:T(8,128)(2,1)S(1)} %all_to_all.23.back_ref, f32[8,128,128]{2,1,0:T(8,128)S(1)} %get-tuple-element.73.pass_ref, f32[8,128,128]{2,1,0:T(8,128)S(1)} %get-tuple-element.74.gates_ref, f32[2,2,128,128]{3,2,1,0:T(8,128)S(1)} %get-tuple-element.60.columns_ref, bf16[2,128,128]{2,1,0:T(8,128)(2,1)S(1)} %copy-done.3), custom_call_target="tpu_custom_call" | custom-call | tf_op jit(solution)/shard_map/finish/pallas_call | solution.py:402
Async XLA Ops:
  2.1 31.8 %copy-start.1 = (bf16[2,128,256]{2,1,0:T(8,128)(2,1)S(1)}, bf16[2,128,256]{2,1,0:T(8,128)(2,1)}, u32[]{:S(2)}) copy-start(bf16[2,128,256]{2,1,0:T(8,128)(2,1)} %proj_in.1) | copy-start | bytes 393220
  2.2 31.8 %copy-start.2 = (bf16[2,128,256]{2,1,0:T(8,128)(2,1)S(1)}, bf16[2,128,256]{2,1,0:T(8,128)(2,1)}, u32[]{:S(2)}) copy-start(bf16[2,128,256]{2,1,0:T(8,128)(2,1)} %gate_in.1) | copy-start | bytes 393220
  2.2 31.8 %copy-start.4 = (bf16[2,128,128]{2,1,0:T(8,128)(2,1)S(1)}, bf16[2,128,128]{2,1,0:T(8,128)(2,1)}, u32[]{:S(2)}) copy-start(bf16[2,128,128]{2,1,0:T(8,128)(2,1)} %gate_out.3) | copy-start | bytes 196612
  31.0 3.0 %copy-start = (f32[64,16,128]{2,1,0:T(8,128)S(1)}, f32[64,16,128]{2,1,0:T(8,128)}, u32[]{:S(2)}) copy-start(f32[64,16,128]{2,1,0:T(8,128)} %param.10) | copy-start | bytes 1572868
  31.8 3.3 %collective-permute-start = (bf16[8,2,16,512]{3,2,1,0:T(8,128)(2,1)S(1)}, bf16[8,2,16,512]{3,2,1,0:T(8,128)(2,1)S(1)}, u32[]{:S(2)}, u32[]{:S(2)}) collective-permute-start(bf16[8,2,16,512]{3,2,1,0:T(8,128)(2,1)S(1)} %get-tuple-element.48), channel_id=1, source_target_pairs={{0,1},{1,0},{2,3},{3,2},{4,5},{5,4},{6,7},{7,6},{8,9},{9,8},{10,11... | collective-permute-start | bytes 786440 | tf_op jit(solution)/shard_map/ppermute | solution.py:312
  35.3 19.2 %copy-start.3 = (bf16[2,128,128]{2,1,0:T(8,128)(2,1)S(1)}, bf16[2,128,128]{2,1,0:T(8,128)(2,1)}, u32[]{:S(2)}) copy-start(bf16[2,128,128]{2,1,0:T(8,128)(2,1)} %proj_out.3) | copy-start | bytes 196612
  78.9 4.5 %collective-permute-start.1 = (bf16[8,2,16,512]{3,2,1,0:T(8,128)(2,1)S(1)}, bf16[8,2,16,512]{3,2,1,0:T(8,128)(2,1)S(1)}, u32[]{:S(2)}, u32[]{:S(2)}) collective-permute-start(bf16[8,2,16,512]{3,2,1,0:T(8,128)(2,1)S(1)} %incoming_left.1.left_ref), channel_id=1, source_target_pairs={{0,1},{1,0},{2,3},{3,2},{4,5},{5,4},{6,7},{7,6},{8,9},{9,8},{10,11... | collective-permute-start | bytes 786440 | tf_op jit(solution)/shard_map/ppermute | solution.py:312
